TPU v7x, 32 devices: a whole 2x2x4 slice. The times are simulated.
32 devices in a mesh: fsdp: 16 (over z, y, core), seq: 2 (over x).
Axes of the slice: x: 2, y: 2, z: 4, core: 2. Of those that a mesh axis runs over, the one named last changes fastest.
Arguments:
- tokens: bfloat16 [16, 1024, 1536], P('fsdp', 'seq'), may hold values from -6 to 6
- segments: int32 [16, 1024], P('fsdp', 'seq'), may hold values from 0 to 4, as said below
- norm_gain: bfloat16 [1536], P(('fsdp', 'seq')), may hold values from 0.5 to 1.5
- in_weight: bfloat16 [1536, 6448], P(('fsdp', 'seq')), may hold values from -0.15625 to 0.15625
- conv_weight: bfloat16 [3328, 4], P(('fsdp', 'seq')), may hold values from -3 to 3
- conv_bias: bfloat16 [3328], P(('fsdp', 'seq')), may hold values from -1.5 to 1.5
- dt_bias: float32 [48], replicated, may hold values from -7 to -2
- a_log: float32 [48], replicated, may hold values from -4 to 1
- d_skip: float32 [48], replicated, may hold values from 0.5 to 1.5
- gated_gain: bfloat16 [3072], P(('fsdp', 'seq')), may hold values from 0.5 to 1.5
- out_weight: bfloat16 [3072, 1536], P(('fsdp', 'seq')), may hold values from -0.109375 to 0.109375
- cotangent: bfloat16 [16, 1024, 1536], P('fsdp', 'seq'), may hold values from -6 to 6
Outputs:
- block_out: bfloat16 [16, 1024, 1536], P('fsdp', 'seq')
- input_grad: float32 [16, 1024, 1536], P('fsdp', 'seq')
- norm_gain_grad: float32 [1536], P(('fsdp', 'seq'))
- in_weight_grad: float32 [1536, 6448], P(('fsdp', 'seq'))
- conv_weight_grad: float32 [3328, 4], P(('fsdp', 'seq'))
- conv_bias_grad: float32 [3328], P(('fsdp', 'seq'))
- dt_bias_grad: float32 [48], replicated
- a_log_grad: float32 [48], replicated
- d_skip_grad: float32 [48], replicated
- gated_gain_grad: float32 [3072], P(('fsdp', 'seq'))
- out_weight_grad: float32 [3072, 1536], P(('fsdp', 'seq'))
Inputs may be any that keep to these rules, and one draw needn't show every extreme that they name: `segments`: within a sequence the numbers start at 0 and never fall, each sequence holds five documents of 102 tokens or more, and in every sequence one document runs from its first piece of 512 tokens into its last.
All inputs are finite; a program needn't handle non-finite values.
Results may differ from a plain program's by a relative error of at most 0.011.
Values may be sent and summed in bfloat16 or wider, within the bound.
No kernel may reach another device: no remote copies, remote signals or barrier semaphores. Data moves between devices by JAX's collectives and lax.ppermute only.
A program may use at most 144 MiB of HBM per device.

v0:
```python
import jax
import jax.numpy as jnp
from jax import lax
from jax.sharding import PartitionSpec as P

NH = 48
HD = 64
NS = 128
KW = 4
SPAN = 256
DI = 3072
CONV = 3328


EPS = 1e-05
HIGH = lax.Precision.HIGHEST


def from_behind(value, axis, by):
    count = lax.axis_size(axis)
    pairs = [(i, i + by) for i in range(count) if 0 <= i + by < count]
    return lax.ppermute(value, axis, pairs)


def prefix(part, axis, combine, identity):
    place = lax.axis_index(axis)
    gathered = jax.tree.map(lambda a: lax.all_gather(a, axis), part)
    state = jax.tree.map(lambda a, e: jnp.zeros_like(a) + jnp.asarray(e, a.dtype), part, identity)

    def prefix_one(lap, state):
        return combine(
            state, jax.tree.map(lambda a: lax.dynamic_index_in_dim(a, lap, 0, False), gathered)
        )

    return lax.fori_loop(0, place, prefix_one, state)


def carried_in(value, axis, join, neutral):
    count = lax.axis_size(axis)
    place = lax.axis_index(axis)
    ahead = count - 1 - place
    gathered = jax.tree.map(
        lambda a, kind: lax.all_gather(a.astype(kind), axis),
        value,
        jax.tree.map(lambda a: jnp.bfloat16 if a.dtype == jnp.float32 else a.dtype, value),
    )
    state = jax.tree.map(lambda a, e: jnp.zeros_like(a) + jnp.asarray(e, a.dtype), value, neutral)

    def carried_one(lap, state):
        source = count - 1 - lap
        return join(
            state,
            jax.tree.map(
                lambda a, own: lax.dynamic_index_in_dim(a, source, 0, False).astype(own.dtype),
                gathered,
                value,
            ),
        )

    return lax.fori_loop(0, ahead, carried_one, state)


def rms_scale(values, gain):
    return values * lax.rsqrt(jnp.mean(values * values, axis=-1, keepdims=True) + EPS) * gain


def join_states(early, late):
    first_a, last_a, decay_a, state_a = early
    first_b, last_b, decay_b, state_b = late
    joined = ((last_a == first_b) | (last_a < 0) | (first_b < 0)).astype(jnp.float32)
    link = decay_b * joined
    return (
        jnp.where(first_a < 0, first_b, first_a),
        jnp.where(last_b < 0, last_a, last_b),
        decay_a * link,
        state_b + link[:, None, None] * state_a,
    )


def join_grads(early, late):
    decay_a, grad_a = early
    decay_b, grad_b = late
    return (decay_a * decay_b, grad_b + decay_b[:, None, None] * grad_a)


def block_step(state, before, seg_blk, x_blk, b_blk, c_blk, dt_blk, dec_blk):
    size = seg_blk.shape[0]
    order = jnp.arange(size)
    lower = order[:, None] >= order[None, :]
    cum_blk = jnp.cumsum(dec_blk, axis=0)
    inside = ((seg_blk[:, None] == seg_blk[None, :]) & lower).astype(jnp.float32)
    spread = cum_blk.T[:, :, None] - cum_blk.T[:, None, :]
    decay = jnp.exp(jnp.where(inside[None] > 0, spread, 0.0)) * inside[None]
    scores = jnp.dot(c_blk, b_blk.T, precision=HIGH)
    mixing = decay * scores[None] * dt_blk.T[:, None, :]
    result = jnp.einsum("hij,jhp->ihp", mixing, x_blk, precision=HIGH)
    keep = (seg_blk == before).astype(jnp.float32)[:, None] * jnp.exp(cum_blk)
    result = result + jnp.einsum("in,hpn->ihp", c_blk, state, precision=HIGH) * keep[:, :, None]
    final = seg_blk[-1]
    tail = (
        (seg_blk == final).astype(jnp.float32)[:, None] * jnp.exp(cum_blk[-1:] - cum_blk) * dt_blk
    )
    fresh = jnp.einsum("jh,jhp,jn->hpn", tail, x_blk, b_blk, precision=HIGH)
    carry_on = (final == before).astype(jnp.float32) * jnp.exp(cum_blk[-1])
    state = carry_on[:, None, None] * state + fresh
    return (result, state, final)


def body(
    tokens,
    segments,
    norm_gain,
    in_weight,
    conv_weight,
    conv_bias,
    dt_bias,
    a_log,
    d_skip,
    gated_gain,
    out_weight,
    cotangent,
):
    rows = tokens.shape[1]
    gathered = (
        lax.all_gather(in_weight, ("fsdp", "seq"), axis=0, tiled=True),
        lax.all_gather(out_weight, ("fsdp", "seq"), axis=0, tiled=True),
        lax.all_gather(norm_gain, ("fsdp", "seq"), axis=0, tiled=True),
        lax.all_gather(gated_gain, ("fsdp", "seq"), axis=0, tiled=True),
        lax.all_gather(conv_weight, ("fsdp", "seq"), axis=0, tiled=True),
        lax.all_gather(conv_bias, ("fsdp", "seq"), axis=0, tiled=True),
    )
    in_full, out_full, gain_low, gated_low, conv_full, bias_full = gathered
    x_local = tokens[0].astype(jnp.float32)
    seg_local = segments[0].astype(jnp.float32)
    normed, pull_norm = jax.vjp(rms_scale, x_local, gain_low.astype(jnp.float32))
    normed_low = normed.astype(jnp.bfloat16)
    proj = jnp.dot(normed_low, in_full, preferred_element_type=jnp.float32).astype(jnp.bfloat16)
    gate_z = proj[:, :DI].astype(jnp.float32)
    xbc = proj[:, DI : DI + CONV]
    raw_dt = proj[:, DI + CONV :].astype(jnp.float32)
    edge_in, edge_seg = from_behind(
        (xbc[rows - KW + 1 :], seg_local[rows - KW + 1 :].astype(jnp.bfloat16)), "seq", 1
    )
    ext_rows = jnp.concatenate([edge_in, xbc], axis=0).astype(jnp.float32)
    ext_seg = jnp.concatenate([edge_seg.astype(jnp.float32), seg_local])

    def conv_mix(ext_in, conv_w, conv_b, dt_raw, bias, alog):
        total = conv_b + jnp.zeros((rows, CONV), jnp.float32)
        for offset in range(KW):
            same = (ext_seg[offset : offset + rows] == seg_local).astype(jnp.float32)
            total = total + ext_in[offset : offset + rows] * conv_w[:, offset] * same[:, None]
        act = jax.nn.silu(total)
        step_dt = jax.nn.softplus(dt_raw + bias)
        return (
            act[:, :DI].reshape(rows, NH, HD),
            act[:, DI : DI + NS],
            act[:, DI + NS :],
            step_dt,
            -jnp.exp(alog) * step_dt,
        )

    mixed, pull_mix = jax.vjp(
        conv_mix,
        ext_rows,
        conv_full.astype(jnp.float32),
        bias_full.astype(jnp.float32),
        raw_dt,
        dt_bias,
        a_log,
    )
    x_heads, b_proj, c_proj, step_dt, log_decay = mixed
    stepper = jax.checkpoint(block_step)

    def piece_scan(heads_in, b_in, c_in, dt_in, decay_in):
        state = jnp.zeros((NH, HD, NS), jnp.float32)
        before = jnp.float32(-1.0)
        outputs = []
        for block in range(rows // SPAN):
            lo_row = block * SPAN
            hi_row = lo_row + SPAN
            result, state, before = stepper(
                state,
                before,
                seg_local[lo_row:hi_row],
                heads_in[lo_row:hi_row],
                b_in[lo_row:hi_row],
                c_in[lo_row:hi_row],
                dt_in[lo_row:hi_row],
                decay_in[lo_row:hi_row],
            )
            outputs.append(result)
        return (jnp.concatenate(outputs, axis=0), state, jnp.cumsum(decay_in, axis=0))

    scanned, pull_scan = jax.vjp(piece_scan, x_heads, b_proj, c_proj, step_dt, log_decay)
    y_local, state_end, cum_all = scanned
    first_seg = seg_local[:1]
    last_seg = seg_local[rows - 1 :]
    whole = (first_seg == last_seg).astype(jnp.float32)
    decay_piece = jnp.exp(cum_all[-1]) * whole
    prior = prefix(
        (first_seg, last_seg, decay_piece, state_end),
        "seq",
        join_states,
        (
            jnp.full((1,), -1.0, jnp.float32),
            jnp.full((1,), -1.0, jnp.float32),
            jnp.ones((NH,), jnp.float32),
            jnp.zeros((NH, HD, NS), jnp.float32),
        ),
    )
    seen_seg = prior[1]
    incoming = prior[3]
    weight_in = (seg_local == seen_seg).astype(jnp.float32)[:, None] * jnp.exp(cum_all)
    from_prior = jnp.einsum("in,hpn->ihp", c_proj, incoming, precision=HIGH)
    y_total = y_local + weight_in[:, :, None] * from_prior

    def gate_norm(y_in, heads_in, skip, gate, gain):
        joined = (y_in + skip[:, None] * heads_in).reshape(rows, DI)
        return rms_scale(joined * jax.nn.silu(gate), gain)

    normed_two, pull_gate = jax.vjp(
        gate_norm, y_total, x_heads, d_skip, gate_z, gated_low.astype(jnp.float32)
    )
    two_low = normed_two.astype(jnp.bfloat16)
    branch = jnp.dot(two_low, out_full, preferred_element_type=jnp.float32)
    block_out = (x_local + branch).astype(jnp.bfloat16)[None]
    in_back, out_back = (
        lax.all_gather(in_weight, ("fsdp", "seq"), axis=0, tiled=True),
        lax.all_gather(out_weight, ("fsdp", "seq"), axis=0, tiled=True),
    )
    cot_local = cotangent[0]
    d_two = lax.dot_general(
        cot_local, out_back, (((1,), (1,)), ((), ())), preferred_element_type=jnp.float32
    )
    d_out_w = lax.dot_general(
        two_low, cot_local, (((0,), (0,)), ((), ())), preferred_element_type=jnp.float32
    )
    d_y, d_heads_gate, d_skip_part, d_gate, d_gain_two = pull_gate(d_two)
    scaled = weight_in[:, :, None] * d_y
    back_state = jnp.einsum("ihp,in->hpn", scaled, c_proj, precision=HIGH)
    d_c_prior = jnp.einsum("ihp,hpn->in", scaled, incoming, precision=HIGH)
    d_cum = jnp.sum(scaled * from_prior, axis=2)
    link_self = decay_piece * (seen_seg == first_seg).astype(jnp.float32)
    later = carried_in(
        (link_self, back_state),
        "seq",
        join_grads,
        (jnp.ones((NH,), jnp.float32), jnp.zeros((NH, HD, NS), jnp.float32)),
    )
    onward = later[1]
    d_link = jnp.sum(onward * incoming, axis=(1, 2))
    d_cum = jnp.concatenate([d_cum[:-1], d_cum[-1:] + (d_link * link_self)[None]], axis=0)
    d_heads_scan, d_b, d_c_scan, d_dt, d_decay = pull_scan((d_y, onward, d_cum))
    d_ext, d_conv_w, d_conv_b, d_raw, d_bias, d_alog = pull_mix(
        (d_heads_scan + d_heads_gate, d_b, d_c_scan + d_c_prior, d_dt, d_decay)
    )
    back_edge = from_behind(d_ext[: KW - 1].astype(jnp.bfloat16), "seq", -1).astype(jnp.float32)
    d_xbc = d_ext[KW - 1 :] + jnp.concatenate(
        [jnp.zeros((rows - KW + 1, CONV), jnp.float32), back_edge], axis=0
    )
    d_proj = jnp.concatenate([d_gate, d_xbc, d_raw], axis=1).astype(jnp.bfloat16)
    d_in_w = lax.dot_general(
        normed_low, d_proj, (((0,), (0,)), ((), ())), preferred_element_type=jnp.float32
    )
    d_normed = lax.dot_general(
        d_proj, in_back, (((1,), (1,)), ((), ())), preferred_element_type=jnp.float32
    )
    d_x, d_gain_one = pull_norm(d_normed)
    input_grad = (cot_local.astype(jnp.float32) + d_x)[None]
    head_grads = lax.psum((d_bias, d_alog, d_skip_part), ("fsdp", "seq"))
    shards = (
        lax.psum_scatter(d_gain_one, ("fsdp", "seq"), scatter_dimension=0, tiled=True),
        lax.psum_scatter(d_in_w, ("fsdp", "seq"), scatter_dimension=0, tiled=True),
        lax.psum_scatter(d_conv_w, ("fsdp", "seq"), scatter_dimension=0, tiled=True),
        lax.psum_scatter(d_conv_b, ("fsdp", "seq"), scatter_dimension=0, tiled=True),
        lax.psum_scatter(d_gain_two, ("fsdp", "seq"), scatter_dimension=0, tiled=True),
        lax.psum_scatter(d_out_w, ("fsdp", "seq"), scatter_dimension=0, tiled=True),
    )
    gain_one_sh, in_sh, conv_w_sh, conv_b_sh, gain_two_sh, out_sh = shards
    return (
        block_out,
        input_grad,
        gain_one_sh,
        in_sh,
        conv_w_sh,
        conv_b_sh,
        head_grads[0],
        head_grads[1],
        head_grads[2],
        gain_two_sh,
        out_sh,
    )


def solution(mesh):
    in_specs = (
        P("fsdp", "seq", None),
        P("fsdp", "seq"),
        P(("fsdp", "seq")),
        P(("fsdp", "seq"), None),
        P(("fsdp", "seq"), None),
        P(("fsdp", "seq")),
        P(),
        P(),
        P(),
        P(("fsdp", "seq")),
        P(("fsdp", "seq"), None),
        P("fsdp", "seq", None),
    )
    out_specs = (
        P("fsdp", "seq", None),
        P("fsdp", "seq", None),
        P(("fsdp", "seq")),
        P(("fsdp", "seq"), None),
        P(("fsdp", "seq"), None),
        P(("fsdp", "seq")),
        P(),
        P(),
        P(),
        P(("fsdp", "seq")),
        P(("fsdp", "seq"), None),
    )
    return jax.shard_map(body, mesh=mesh, in_specs=in_specs, out_specs=out_specs, check_vma=False)
```

profile of v0, /device:TPU:0, one launch (start us, length us, event | category | flops | bytes accessed | tf_op | source)
XLA Modules:
  0.0 1419.9 jit_solution(3834653776425747553)
XLA Ops:
  18.7 41.0 %all-reduce.37 = (bf16[1536]{0:T(1024)(128)(2,1)S(1)}, bf16[3328]{0:T(1024)(128)(2,1)S(1)}, bf16[3072]{0:T(1024)(128)(2,1)}) all-reduce(bf16[1536]{0:T(1024)(128)(2,1)S(1)} %dynamic-update-slice.1, bf16[3328]{0:T(1024)(128)(2,1)S(1)} %dynamic-update-slice, ...), channel_id=1, replica_groups=mesh['fsdp'=16,'seq'=2] {'fsdp','seq'}, use_global_device_ids=true, to_apply=%add.27 | all-reduce | flops 7936 | bytes 31744
  60.3 67.8 %all-gather.2 = bf16[32,104,4]{1,2,0:T(4,128)(2,1)S(1)} all-gather(bf16[1,104,4]{1,2,0:T(4,128)(2,1)} %bitcast.403), channel_id=1, replica_groups=mesh['fsdp'=16,'seq'=2] {'fsdp','seq'}, dimensions={0}, use_global_device_ids=true | all-gather | bytes 27456 | tf_op jit(solution)/shard_map/all_gather | solution.py:129
  135.4 10.1 all-gather.10.cloned.1.call-done
  145.5 15.4 %convolution_convert_fusion = bf16[512,6448]{1,0:T(8,128)(2,1)S(1)} fusion(bf16[1536,6448]{1,0:T(8,128)(2,1)} %all-gather.10.cloned.1.call-done, bf16[1,512,1536]{2,1,0:T(8,128)(2,1)} %param.16, f32[1536]{0:T(1024)S(1)} %convert_element_type.202, f32[512]{0:T(512)S(1)} %fusion.195), kind=kOutput, calls=%fused_computation.38 | convolution fusion | flops 10148274176 | bytes 27992064 | tf_op jit(solution)/shard_map/dot_general | solution.py:137
  195.6 8.0 fusion.29
  266.3 15.8 %bitcast_add_fusion.4 = f32[256,48,64]{0,2,1:T(8,128)} fusion(f32[256,48,64]{0,2,1:T(8,128)S(1)} %fusion.160, f32[256,48,64]{0,2,1:T(8,128)S(1)} %bitcast.338, f32[48,256]{1,0:T(8,128)S(1)} %copy-done.84, f32[256,256]{1,0:T(8,128)S(1)} %fusion.213, f32[256,256]{1,0:T(8,128)S(1)} %get-tuple-element.342, f32[48,256]{1,0:T(8,128)S(1)} %copy-done.83, ...), kind=kOutput, calls=%fused_computation.137 | convolution fusion | flops 2433220608 | bytes 10174464 | tf_op jit(solution)/shard_map/jvp(hij,jhp->ihp)/dot_general | solution.py:96
  282.1 15.9 %bitcast_add_fusion.3 = f32[256,48,64]{0,2,1:T(8,128)} fusion(f32[256,48,64]{0,2,1:T(8,128)S(1)} %fusion.186, f32[256,48,64]{0,2,1:T(8,128)S(1)} %bitcast.343, f32[48,256]{1,0:T(8,128)S(1)} %copy.369, f32[256,256]{1,0:T(8,128)S(1)} %fusion.208, f32[256,256]{1,0:T(8,128)S(1)} %get-tuple-element.344, f32[48,256]{1,0:T(8,128)S(1)} %copy.367, ...), kind=kOutput, calls=%fused_computation.136 | convolution fusion | flops 2433220608 | bytes 10174464 | tf_op jit(solution)/shard_map/jvp(hij,jhp->ihp)/dot_general | solution.py:96
  298.9 11.5 fusion.40
  317.1 7.6 multiply_reduce_fusion.12
  324.7 28.0 %all-gather.12.cloned.1.call-done = bf16[3072,1536]{1,0:T(8,128)(2,1)} async-done(((bf16[96,1536]{1,0:T(8,128)(2,1)}), bf16[3072,1536]{1,0:T(8,128)(2,1)}) %all-gather.12.cloned.1.call-update) | async-done | bytes 9437200 | tf_op jit(solution)/shard_map/all_gather | solution.py:126
  352.7 12.5 multiply_reduce_fusion.8
  365.3 10.6 multiply_reduce_fusion.9
  382.4 8.3 fusion.139
  448.4 20.6 %fusion.31 = (f32[48,256]{1,0:T(8,128)}, f32[48,256]{1,0:T(8,128)}, f32[48,256]{1,0:T(8,128)}, f32[256,256]{1,0:T(8,128)}) fusion(f32[256,256]{1,0:T(8,128)S(1)} %fusion.229, f32[48,256]{1,0:T(8,128)S(1)} %copy-done.79, f32[256,256]{1,0:T(8,128)S(1)} %copy-done.57, f32[48,256]{1,0:T(8,128)S(1)} %copy-done.80, pred[256,256]{1,0:T(8,128)(4,1)S(1)} %copy-done.71, ...), kind=kOutput, calls=%fused_computation.59 | convolution fusion | flops 2463002624 | bytes 7389184 | tf_op jit(solution)/shard_map/transpose(jvp(jvp()))/checkpoint/hij,jhp->ihp/dot_general | solution.py:96
  479.3 8.2 fusion.148
  498.1 7.8 fusion.154
  506.0 14.2 %bitcast_add_fusion.2 = f32[256,48,64]{0,2,1:T(8,128)} fusion(f32[256,48,64]{0,2,1:T(8,128)} %get-tuple-element.349, f32[256,256]{1,0:T(8,128)} %copy-done.58, f32[48,256]{1,0:T(8,128)} %copy.385, f32[256,256]{1,0:T(8,128)} %get-tuple-element.332, f32[48,256]{1,0:T(8,128)} %copy.383, pred[256,256]{1,0:T(8,128)(4,1)} %get-tuple-element.331, ...), kind=kOutput, calls=%fused_computation.129 | convolution fusion | flops 2433220608 | bytes 10174464 | tf_op jit(solution)/shard_map/transpose(jvp(jvp()))/checkpoint/hij,jhp->ihp/dot_general | solution.py:96
  539.0 7.3 multiply_reduce_fusion.13
  546.3 20.6 %fusion.33 = (f32[48,256]{1,0:T(8,128)}, f32[48,256]{1,0:T(8,128)}, f32[48,256]{1,0:T(8,128)}, f32[256,256]{1,0:T(8,128)}) fusion(f32[256,256]{1,0:T(8,128)S(1)} %fusion.230, f32[48,256]{1,0:T(8,128)S(1)} %copy-done.81, f32[256,256]{1,0:T(8,128)S(1)} %copy-done.56, f32[48,256]{1,0:T(8,128)S(1)} %copy-done.82, pred[256,256]{1,0:T(8,128)(4,1)S(1)} %copy-done.70, ...), kind=kOutput, calls=%fused_computation.61 | convolution fusion | flops 2463002624 | bytes 7389184 | tf_op jit(solution)/shard_map/transpose(jvp(jvp()))/checkpoint/hij,jhp->ihp/dot_general | solution.py:96
  576.8 8.2 fusion.157
  585.0 13.3 bitcast_add_fusion.1
  613.8 7.1 fusion.151
  624.3 12.2 fusion.145
  636.7 12.0 multiply_reduce_fusion.7
  658.1 8.2 multiply_multiply_fusion.3
  679.3 19.8 %fusion.76 = (f32[1536]{0:T(1024)}, f32[512]{0:T(512)S(1)}, f32[512,1536]{1,0:T(8,128)}) fusion(bf16[1,512,1536]{2,1,0:T(8,128)(2,1)S(1)} %copy-done.16, f32[512]{0:T(512)S(1)} %copy-done.54, f32[1536]{0:T(1024)S(1)} %copy-done.37, bf16[1536,6448]{1,0:T(8,128)(2,1)} %all-gather.10.cloned.1.call-done, bf16[512,48]{1,0:T(8,128)(2,1)S(1)} %get-tuple-element.270, ...), kind=kOutput, calls=%fused_computation.123 | convolution fusion | flops 10167138304 | bytes 31145984 | tf_op jit(solution)/shard_map/dot_general | solution.py:265
  699.2 12.4 fusion.121
  711.7 21.4 %fusion.106 = f32[1536,6448]{1,0:T(8,128)} fusion(bf16[512,48]{1,0:T(8,128)(2,1)S(1)} %get-tuple-element.270, bf16[512,3328]{1,0:T(8,128)(2,1)} %copy-done.17, bf16[512,3072]{1,0:T(8,128)(2,1)} %get-tuple-element.278, bf16[1,512,1536]{2,1,0:T(8,128)(2,1)S(1)} %copy-done.16, f32[1536]{0:T(1024)S(1)} %copy-done.37, f32[512]{0:T(512)S(1)} %copy-done.54), kind=kOutput, calls=%fused_computation.161 | convolution fusion | flops 10164781056 | bytes 47800320 | tf_op jit(solution)/shard_map/dot_general | solution.py:262
  733.2 11.0 fusion.105
  746.8 76.8 %all-reduce.40.cloned.1.call-done = (f32[1536]{0:T(1024)}, f32[3328,4]{0,1:T(4,128)}, f32[3328]{0:T(1024)}, f32[48]{0:T(128)}, f32[48]{0:T(128)}, /*index=5*/f32[48]{0:T(128)}, f32[3072]{0:T(1024)}) async-done(((f32[1536]{0:T(1024)}, f32[3328,4]{0,1:T(4,128)}, f32[3328]{0:T(1024)}, f32[48]{0:T(128)}, f32[48]{0:T(128)}, /*index=5*/f32[48]{0:T(128)}, f32[3072]{0:T(1024)}), (f32[1536]{0:T(1024)}, ...) | async-done | bytes 85584
  828.7 209.5 %reduce-scatter.6.cloned.1.call-done = f32[96,1536]{1,0:T(8,128)} async-done(((f32[3072,1536]{1,0:T(8,128)}), f32[96,1536]{1,0:T(8,128)}) %reduce-scatter.6.cloned.1.call-update) | async-done | bytes 589840 | tf_op jit(solution)/shard_map/reduce_scatter | solution.py:277
  1038.2 371.2 %reduce-scatter.4.cloned.1.call-done = f32[48,6448]{1,0:T(8,128)} async-done(((f32[1536,6448]{1,0:T(8,128)}), f32[48,6448]{1,0:T(8,128)}) %reduce-scatter.4.cloned.1.call-update) | async-done | bytes 1238032 | tf_op jit(solution)/shard_map/reduce_scatter | solution.py:273
  (465 shorter events, 285.0 us)
Async XLA Ops:
  7.2 138.3 %all-gather.10.cloned.1.call-start = ((), (), s32[]{:S(2)}) async-start(), calls=%async_computation.2 | async-start | bytes 20680704 | tf_op jit(solution)/shard_map/all_gather | solution.py:125
  7.9 290.0 %all-gather.14.cloned.1.call-start = ((), (), s32[]{:S(2)}) async-start(), calls=%async_computation.6 | async-start | bytes 4718592 | tf_op jit(solution)/shard_map/all_gather | solution.py:27
  8.6 152.3 %copy-start.68 = (f32[1,512]{1,0:T(1,128)}, f32[1,512]{1,0:T(1,128)S(1)}, u32[]{:S(2)}) copy-start(f32[1,512]{1,0:T(1,128)S(1)} %convert_element_type.207) | copy-start | bytes 6148
  8.7 125.9 %collective-permute-start.1 = (bf16[3]{0:T(256)(128)(2,1)S(1)}, bf16[3]{0:T(256)(128)(2,1)S(1)}, u32[]{:S(2)}, u32[]{:S(2)}) collective-permute-start(bf16[3]{0:T(256)(128)(2,1)S(1)} %fusion.197), channel_id=1, source_target_pairs={{0,1},{2,3},{4,5},{6,7},{8,9},{10,11},{12,13},{14,15},{16,17},{18,... | collective-permute-start | bytes 26 | tf_op jit(solution)/shard_map/ppermute | solution.py:22
  59.7 101.3 %copy-start.36 = (f32[1536]{0:T(1024)}, f32[1536]{0:T(1024)S(1)}, u32[]{:S(2)}) copy-start(f32[1536]{0:T(1024)S(1)} %convert_element_type.202) | copy-start | bytes 18436
  129.0 66.6 %copy-start.62 = (f32[3328]{0:T(1024)}, f32[3328]{0:T(1024)S(1)}, u32[]{:S(2)}) copy-start(f32[3328]{0:T(1024)S(1)} %get-tuple-element.225) | copy-start | bytes 39940
  131.5 34.0 %copy-start.102 = (f32[48]{0:T(128)}, f32[48]{0:T(128)S(1)}, u32[]{:S(2)}) copy-start(f32[48]{0:T(128)S(1)} %exponential_negate_fusion) | copy-start | bytes 580
  131.5 29.5 %copy-start.75 = (f32[1,256]{1,0:T(1,128)}, f32[1,256]{1,0:T(1,128)S(1)}, u32[]{:S(2)}) copy-start(f32[1,256]{1,0:T(1,128)S(1)} %get-tuple-element.326) | copy-start | bytes 3076
  134.6 26.4 %copy-start.53 = (f32[512]{0:T(512)}, f32[512]{0:T(512)S(1)}, u32[]{:S(2)}) copy-start(f32[512]{0:T(512)S(1)} %fusion.195) | copy-start | bytes 6148
  135.4 30.2 %copy-start.100 = (f32[48]{0:T(128)S(1)}, f32[48]{0:T(128)}, u32[]{:S(2)}) copy-start(f32[48]{0:T(128)} %param.22) | copy-start | bytes 580
  161.7 32.4 %collective-permute-start = (bf16[3,3328]{1,0:T(4,128)(2,1)}, bf16[3,3328]{1,0:T(4,128)(2,1)}, u32[]{:S(2)}, u32[]{:S(2)}) collective-permute-start(bf16[3,3328]{1,0:T(4,128)(2,1)} %slice.285), channel_id=1, source_target_pairs={{0,1},{2,3},{4,5},{6,7},{8,9},{10,11},{12,13},{14,15},{16,17},{18,... | collective-permute-start | bytes 59912 | tf_op jit(solution)/shard_map/ppermute | solution.py:22
  166.4 27.7 %slice-start.6 = ((bf16[512,6448]{1,0:T(8,128)(2,1)}), bf16[512,3328]{1,0:T(8,128)(2,1)S(1)}, s32[]{:S(2)}) async-start(bf16[512,6448]{1,0:T(8,128)(2,1)} %copy-done.15), calls=%async_computation.15 | async-start | bytes 6815744 | tf_op jit(solution)/shard_map/slice | solution.py:139
  189.7 240.2 %copy-start.27 = (f32[256,48]{1,0:T(8,128)}, f32[256,48]{1,0:T(8,128)S(1)}, u32[]{:S(2)}) copy-start(f32[256,48]{1,0:T(8,128)S(1)} %get-tuple-element.194) | copy-start | bytes 147460
  214.9 22.2 %copy-start.31 = (f32[48,2,128]{0,2,1:T(8,128)S(1)}, f32[48,2,128]{0,2,1:T(8,128)}, u32[]{:S(2)}) copy-start(f32[48,2,128]{0,2,1:T(8,128)} %copy-done.30) | copy-start | bytes 147460
  214.9 22.3 %copy-start.32 = (f32[48,2,128]{0,2,1:T(8,128)S(1)}, f32[48,2,128]{0,2,1:T(8,128)}, u32[]{:S(2)}) copy-start(f32[48,2,128]{0,2,1:T(8,128)} %copy.359) | copy-start | bytes 147460
  214.9 23.0 %copy-start.49 = (f32[48,256]{0,1:T(8,128)S(1)}, f32[48,256]{0,1:T(8,128)}, u32[]{:S(2)}) copy-start(f32[48,256]{0,1:T(8,128)} %get-tuple-element.304) | copy-start | bytes 147460
  219.6 43.2 %copy-start.3 = (f32[48,64,128]{2,1,0:T(8,128)}, f32[48,64,128]{2,1,0:T(8,128)S(1)}, u32[]{:S(2)}) copy-start(f32[48,64,128]{2,1,0:T(8,128)S(1)} %fusion.134) | copy-start | bytes 4718596
  224.9 127.7 %all-gather.12.cloned.1.call-start = ((), (), s32[]{:S(2)}) async-start(), calls=%async_computation.3 | async-start | bytes 9732096 | tf_op jit(solution)/shard_map/all_gather | solution.py:126
  225.7 191.0 %all-gather.16.cloned.1.call-start = ((), (), s32[]{:S(2)}) async-start(), calls=%async_computation.7 | async-start | bytes 2359296 | tf_op jit(solution)/shard_map/all_gather | solution.py:43
  235.3 130.0 %copy-start.77 = (f32[3072]{0:T(1024)}, f32[3072]{0:T(1024)S(1)}, u32[]{:S(2)}) copy-start(f32[3072]{0:T(1024)S(1)} %convert_element_type.226) | copy-start | bytes 36868
  317.1 35.6 %copy-start.28 = (bf16[1,512,1536]{2,1,0:T(8,128)(2,1)S(1)}, bf16[1,512,1536]{2,1,0:T(8,128)(2,1)}, u32[]{:S(2)}) copy-start(bf16[1,512,1536]{2,1,0:T(8,128)(2,1)} %param.27) | copy-start | bytes 4718596
  324.7 40.5 %copy-start.92 = (f32[512]{0:T(512)}, f32[512]{0:T(512)S(1)}, u32[]{:S(2)}) copy-start(f32[512]{0:T(512)S(1)} %fusion.196) | copy-start | bytes 6148
  390.7 432.9 %all-reduce.40.cloned.1.call-start = ((), (), s32[]{:S(2)}) async-start(), calls=%async_computation.8 | async-start | bytes 183296
  442.4 26.7 %copy-start.58 = (f32[256,256]{1,0:T(8,128)}, f32[256,256]{1,0:T(8,128)S(1)}, u32[]{:S(2)}) copy-start(f32[256,256]{1,0:T(8,128)S(1)} %fusion.229) | copy-start | bytes 786436
  538.9 27.9 %copy-start.59 = (f32[256,256]{1,0:T(8,128)}, f32[256,256]{1,0:T(8,128)S(1)}, u32[]{:S(2)}) copy-start(f32[256,256]{1,0:T(8,128)S(1)} %fusion.230) | copy-start | bytes 786436
  576.8 21.6 %slice-start.2 = ((s8[6291456]{0:T(1024)(128)(4,1)}), s8[4194304]{0:T(1024)(128)(4,1)S(1)}, s32[]{:S(2)}) async-start(s8[6291456]{0:T(1024)(128)(4,1)} %bitcast.332), calls=%async_computation.11 | async-start | bytes 8388608
  576.8 21.6 %slice-start.4 = ((s8[6291456]{0:T(1024)(128)(4,1)}), s8[4194304]{0:T(1024)(128)(4,1)S(1)}, s32[]{:S(2)}) async-start(s8[6291456]{0:T(1024)(128)(4,1)} %bitcast.357), calls=%async_computation.13 | async-start | bytes 8388608
  613.8 22.8 %slice-start = ((s8[6922240]{0:T(1024)(128)(4,1)}), s8[4194304]{0:T(1024)(128)(4,1)S(1)}, s32[]{:S(2)}) async-start(s8[6922240]{0:T(1024)(128)(4,1)} %bitcast.328), calls=%async_computation.9 | async-start | bytes 8388608
  636.7 21.4 %copy-start.63 = (f32[3328]{0:T(1024)S(1)}, f32[3328]{0:T(1024)}, u32[]{:S(2)}) copy-start(f32[3328]{0:T(1024)} %copy-done.62) | copy-start | bytes 39940
  672.6 6.0 collective-permute-start.2
  699.1 339.1 %reduce-scatter.6.cloned.1.call-start = ((), (), s32[]{:S(2)}) async-start(), calls=%async_computation.5 | async-start | bytes 19464192 | tf_op jit(solution)/shard_map/reduce_scatter | solution.py:277
  711.7 697.7 %reduce-scatter.4.cloned.1.call-start = ((), (), s32[]{:S(2)}) async-start(), calls=%async_computation.4 | async-start | bytes 41361408 | tf_op jit(solution)/shard_map/reduce_scatter | solution.py:273
  (95 other events, 1087.7 us)
Sparse Core Ops, SparseCore 0:
  10.9 134.5 all-gather.9
  225.0 42.5 all-gather.13
  270.6 82.0 all-gather.11
  390.8 25.8 all-gather.15
  699.2 124.2 all-reduce.39
  830.4 207.7 reduce-scatter.5
  1045.2 364.1 reduce-scatter.3
where the time goes:
time: 1430 us; the launch traced here: 1420 us
  waiting for transfers between devices  703 us (49%)
  matrix products  311 us (22%)
  other arithmetic  131 us (9%)
  blocking collectives  123 us (9%)
  local copies, waits for them, and re-layouts  120 us (8%)
  between operations  21.9 us (2%)
    reduce_scatter x1, waiting for transfers between devices, body(): lax.psum_scatter(d_in_w, ('fsdp', 'seq'), scatter_dimension=0, tiled=True)  371 us
    reduce_scatter x1, waiting for transfers between devices, body(): lax.psum_scatter(d_out_w, ('fsdp', 'seq'), scatter_dimension=0, tiled=True)  209 us
    dot_general x6, matrix products, block_step(): result = jnp.einsum('hij,jhp->ihp', mixing, x_blk, precision=HIGH)  100 us
    unnamed x8, waiting for transfers between devices  78.2 us
    all_gather x1, blocking collectives, body(): lax.all_gather(conv_weight, ('fsdp', 'seq'), axis=0, tiled=True)  67.8 us
    unnamed x2, blocking collectives  46 us
    dot_general x6, matrix products, block_step(): fresh = jnp.einsum('jh,jhp,jn->hpn', tail, x_blk, b_blk, precision=HIGH)  39.2 us
    dot_general x7, matrix products, block_step(): jnp.einsum('in,hpn->ihp', c_blk, state, precision=HIGH) * keep[:, :, None]  35.3 us
  transfers between devices with their start and end apart: 10, of which 7 were waited for; matrix products, arithmetic and copies ran while one was open for 14% of the time, Pallas kernels for 0%

commit v1 on v0

v1 whole, which is shorter than its diff:
```python
import jax
import jax.numpy as jnp
import numpy as np
from jax import lax
from jax.experimental import pallas as pl
from jax.experimental.pallas import tpu as pltpu
from jax.sharding import Mesh
from jax.sharding import PartitionSpec as P

D = 1536
NH = 48
HD = 64
NS = 128
KW = 4
DI = 3072
CONV = 3328
LEN = 1024

EPS = 1e-05
HIGH = lax.Precision.HIGHEST
F32 = jnp.float32
BF16 = jnp.bfloat16

PARTS = 4
MYH = NH // PARTS
MYC = MYH * HD
BCW = 2 * NS // PARTS
LANES = 128
W1 = MYC + LANES
Q = 128
FAR = -1e30

SWAP = [(0, 1), (1, 0)]


def swap(value, axis):
    return lax.ppermute(value, axis, SWAP)


def pick(value, at, dim=0):
    return lax.dynamic_index_in_dim(value, at, dim, False)


def in_order(mine, other, place):
    buf = jnp.zeros((2,) + mine.shape, mine.dtype)
    buf = lax.dynamic_update_index_in_dim(buf, mine, place, 0)
    return lax.dynamic_update_index_in_dim(buf, other, 1 - place, 0)


def group_gather(value, core, side):
    pair = in_order(value, swap(value, "seq"), side)
    return in_order(pair, swap(pair, "core"), core)


def group_sum(value):
    value = value + swap(value, "core")
    return value + swap(value, "seq")


def group_scatter(value, core, side):
    kept = pick(value, core).astype(F32) + swap(pick(value, 1 - core), "core").astype(F32)
    sent = swap(pick(kept, 1 - side).astype(BF16), "seq")
    return pick(kept, side) + sent.astype(F32)


def ring_order(count):
    return list(range(0, count, 2)) + list(range(count - 1, 0, -2))


def ring_pairs(count):
    order = ring_order(count)
    right = [(order[i], order[(i + 1) % count]) for i in range(count)]
    return right, [(b, a) for a, b in right]


def ring_place(count):
    order = np.array(ring_order(count), np.int32)
    return jnp.asarray(np.argsort(order).astype(np.int32))[lax.axis_index("zy")], jnp.asarray(order)


def ring_gather(block):
    count = lax.axis_size("zy")
    rows = block.shape[0]
    half = rows // 2
    right, left = ring_pairs(count)
    place, order = ring_place(count)

    def put(full, part, at, off=0):
        return lax.dynamic_update_slice(full, part[None], (order[at % count], off, 0))

    full = put(jnp.zeros((count,) + block.shape, block.dtype), block, place)
    ahead = back = block
    for step in range(1, count // 2):
        ahead = lax.ppermute(ahead, "zy", right)
        back = lax.ppermute(back, "zy", left)
        full = put(full, ahead, place - step + count)
        full = put(full, back, place + step)
    ahead = lax.ppermute(ahead[:half], "zy", right)
    back = lax.ppermute(back[half:], "zy", left)
    full = put(full, ahead, place + count // 2)
    return put(full, back, place + count // 2, half)


def ring_scatter(full):
    count, rows, cols = full.shape
    half = rows // 2
    right, left = ring_pairs(count)
    place, order = ring_place(count)

    def get(at, off=0, size=rows):
        return lax.dynamic_slice(full, (order[at % count], off, 0), (1, size, cols))[0].astype(F32)

    far = place + count // 2
    ahead = lax.ppermute(get(far, 0, half).astype(BF16), "zy", right)
    back = lax.ppermute(get(far, half, rows - half).astype(BF16), "zy", left)
    for step in range(count // 2 - 1, 0, -1):
        one, two = get(place + step), get(place + count - step)
        if step == count // 2 - 1:
            one = jnp.concatenate([one[:half] + ahead, one[half:]], axis=0)
            two = jnp.concatenate([two[:half], two[half:] + back], axis=0)
        else:
            one, two = one + ahead, two + back
        ahead = lax.ppermute(one.astype(BF16), "zy", right)
        back = lax.ppermute(two.astype(BF16), "zy", left)
    return get(place) + ahead.astype(F32) + back.astype(F32)


def zy_exchange(value, bit):
    count = lax.axis_size("zy")
    return lax.ppermute(value, "zy", [(i, i ^ bit) for i in range(count)])


def small_gather(value, core, side):
    count = lax.axis_size("zy")
    held = group_gather(value, core, side)[None]
    place = lax.axis_index("zy")
    bit = 1
    while bit < count:
        other = zy_exchange(held, bit)
        upper = (place // bit) % 2
        pair = in_order(held, other, upper)
        held = pair.reshape((2 * bit,) + value.shape[:0] + held.shape[1:])
        bit *= 2
    return held


def zy_sum(value):
    count = lax.axis_size("zy")
    bit = 1
    while bit < count:
        value = value + zy_exchange(value, bit)
        bit *= 2
    return value


def head_split(count):
    rows = DI // count
    if rows % (2 * HD) == 0 and count % 2 == 0:
        return count // 2, rows // (2 * HD)
    return 1, MYH


def split_heads(value, dim, split):
    q, i = split
    size = value.shape[dim]
    unit = size // NH
    shape = value.shape
    value = value.reshape(shape[:dim] + (2, q, 2, i * unit) + shape[dim + 1 :])
    value = jnp.swapaxes(value, dim + 1, dim + 2)
    return value.reshape(shape[:dim] + (2, 2, size // PARTS) + shape[dim + 1 :])


def join_heads(value, dim, split):
    q, i = split
    shape = value.shape
    mine = shape[dim + 2]
    value = value.reshape(shape[:dim] + (2, 2, q, mine // q) + shape[dim + 3 :])
    value = jnp.swapaxes(value, dim + 1, dim + 2)
    return value.reshape(shape[:dim] + (PARTS * mine,) + shape[dim + 3 :])


def split_columns(weight, split):
    rows = weight.shape[0]
    gate = split_heads(weight[:, :DI], 1, split)
    x_cols = split_heads(weight[:, DI : 2 * DI], 1, split)
    bc_cols = weight[:, 2 * DI : 2 * DI + 2 * NS].reshape(rows, 2, 2, BCW)
    dt_cols = split_heads(weight[:, DI + CONV :], 1, split)
    pad = jnp.zeros((rows, 2, 2, LANES - BCW - MYH), weight.dtype)
    first = jnp.concatenate([x_cols, dt_cols, pad, bc_cols], axis=3)
    return jnp.transpose(first, (1, 2, 0, 3)), jnp.transpose(gate, (1, 2, 0, 3))


def join_columns(first, gate, split):
    rows = first.shape[2]
    first = jnp.transpose(first, (2, 0, 1, 3))
    gate = jnp.transpose(gate, (2, 0, 1, 3))
    return jnp.concatenate(
        [
            join_heads(gate, 1, split),
            join_heads(first[..., :MYC], 1, split),
            first[..., W1 - BCW :].reshape(rows, 2 * NS),
            join_heads(first[..., MYC : MYC + MYH], 1, split),
        ],
        axis=1,
    )


def to_group(blocks, core, side):
    kept, got = pick(blocks, core), swap(pick(blocks, 1 - core), "core")
    pair = in_order(kept, got, core)
    kept, got = pick(pair, side, 1), swap(pick(pair, 1 - side, 1), "seq")
    return jnp.swapaxes(in_order(kept, got, side), 0, 1)


def from_group(blocks, core, side):
    kept, got = pick(blocks, side, 1), swap(pick(blocks, 1 - side, 1), "seq")
    pair = in_order(kept, got, side)
    kept, got = pick(pair, core, 1), swap(pick(pair, 1 - core, 1), "core")
    return in_order(kept, got, core)


DIAGONAL = [(0, 0), (1, 2), (2, 1), (3, 3)]


def nt(a, b):
    return lax.dot_general(a, b, (((1,), (1,)), ((), ())), preferred_element_type=F32)


def nn(a, b):
    return lax.dot_general(a, b, (((1,), (0,)), ((), ())), preferred_element_type=F32)


def exact(a, b):
    return lax.dot_general(
        a, b, (((1,), (0,)), ((), ())), preferred_element_type=F32, precision=HIGH
    )


def in_two(value, axis):
    top = value.astype(BF16)
    return jnp.concatenate([top, (value - top.astype(F32)).astype(BF16)], axis=axis)


def over_heads(value, heads_ref):
    return nn(in_two(value, 1), heads_ref[...])


def sum_heads(value, heads_ref):
    top = value.astype(BF16)
    low = (value - top.astype(F32)).astype(BF16)
    heads = heads_ref[:LANES, :]
    return nt(top, heads) + nt(low, heads)


def softplus(value):
    return jnp.maximum(value, 0.0) + jnp.log1p(jnp.exp(-jnp.abs(value)))


def conv_total(ext_ref, raw_ref, halo_ref, taps_ref, marks, width):
    ext_ref[0:8, :width] = halo_ref[8:16, :].astype(F32)
    ext_ref[8 : 8 + Q, :width] = raw_ref[...].astype(F32)
    total = taps_ref[4:5, :] + ext_ref[8 : 8 + Q, :width] * taps_ref[3:4, :]
    for k in range(KW - 1):
        total = total + ext_ref[5 + k : 5 + k + Q, :width] * taps_ref[k : k + 1, :] * marks[:, 1 + k : 2 + k]
    return total


def decays(dt_ref, head_ref, lower):
    raw = dt_ref[...].astype(F32)
    lane = lax.broadcasted_iota(jnp.int32, (Q, LANES), 1)
    live = (lane < MYH).astype(F32)
    shifted = raw * live + head_ref[0:1, :]
    step = softplus(shifted) * live
    rate = -jnp.exp(head_ref[1:2, :])
    log_decay = rate * step
    return shifted, step, rate, log_decay, exact(lower, log_decay)


def scan_forward(
    x_ref, x_halo, bc_ref, bc_halo, dt_ref, marks_ref, row_ref, x_taps, bc_taps, head_ref, heads_ref,
    y_ref, state_ref, bc_out, ext, held,
):
    chunk = pl.program_id(1)

    @pl.when(chunk == 0)
    def _():
        held[...] = jnp.zeros_like(held)

    marks = marks_ref[...]
    x_act = conv_total(ext, x_ref, x_halo, x_taps, marks, MYC)
    x_act = x_act * lax.logistic(x_act)
    bc_act = conv_total(ext, bc_ref, bc_halo, bc_taps, marks, 2 * NS)
    bc_act = (bc_act * lax.logistic(bc_act)).astype(BF16)
    bc_out[...] = bc_act
    b, c = bc_act[:, :NS], bc_act[:, NS:]
    at_row = lax.broadcasted_iota(jnp.int32, (Q, Q), 0)
    at_col = lax.broadcasted_iota(jnp.int32, (Q, Q), 1)
    lower = (at_row >= at_col).astype(F32)
    _, step, _, _, cum = decays(dt_ref, head_ref, lower)
    cum_t = cum.T
    shut = jnp.where((at_row >= at_col) & (marks[:, 0:1] == row_ref[0]), 0.0, FAR)
    scores = nt(c, b)
    state = held[...]
    state_low = state.astype(BF16)
    state_ref[0] = state_low
    last = cum[Q - 1 : Q, :]
    x_step = x_act * over_heads(step, heads_ref)
    keep = over_heads(jnp.exp(cum) * marks[:, 7:8], heads_ref)
    y = nn(c, state_low) * keep + x_act * x_taps[5:6, :]
    tail = over_heads(jnp.exp(last - cum) * marks[:, 8:9], heads_ref)
    carry = over_heads(jnp.broadcast_to(jnp.exp(last) * marks[Q - 1 : Q, 7:8], (8, LANES)), heads_ref)
    held[...] = state * carry[0:1, :] + nn(b.T, (x_step * tail).astype(BF16))
    lane = lax.broadcasted_iota(jnp.int32, (Q, LANES), 1)
    for pair in range(MYH // 2):
        cols = slice(pair * LANES, (pair + 1) * LANES)
        mixing = []
        for head in (2 * pair, 2 * pair + 1):
            spread = cum[:, head : head + 1] - cum_t[head : head + 1, :] + shut
            mixing.append((jnp.exp(spread) * scores).astype(BF16))
        steps = x_step[:, cols]
        both = jnp.concatenate(
            [jnp.where(lane < HD, steps, 0.0), jnp.where(lane < HD, 0.0, steps)], axis=0
        ).astype(BF16)
        y_ref[:, cols] = y[:, cols] + nn(jnp.concatenate(mixing, axis=1), both)


def scan_backward(
    x_ref, x_halo, bc_ref, dt_ref, dy_ref, state_ref, marks_ref, row_ref, x_taps, head_ref, heads_ref,
    dx_ref, dbc_ref, ddt_ref, wide_ref, thin_ref, ext, held, ahead,
):
    chunk = pl.program_id(1)

    @pl.when(chunk == 0)
    def _():
        held[...] = jnp.zeros_like(held)
        ahead[...] = jnp.zeros_like(ahead)

    @pl.when((chunk == 0) & (pl.program_id(0) == 0))
    def _():
        wide_ref[...] = jnp.zeros_like(wide_ref)
        thin_ref[...] = jnp.zeros_like(thin_ref)

    marks = marks_ref[...]
    total = conv_total(ext, x_ref, x_halo, x_taps, marks, MYC)
    gate = lax.logistic(total)
    x_act = total * gate
    slope = gate * (1.0 + total * (1.0 - gate))
    b, c = bc_ref[:, :NS], bc_ref[:, NS:]
    at_row = lax.broadcasted_iota(jnp.int32, (Q, Q), 0)
    at_col = lax.broadcasted_iota(jnp.int32, (Q, Q), 1)
    lower = (at_row >= at_col).astype(F32)
    shifted, step, rate, log_decay, cum = decays(dt_ref, head_ref, lower)
    cum_t = cum.T
    shut = jnp.where((at_row <= at_col) & (marks[:, 0:1] == row_ref[0]), 0.0, FAR)
    scores = nt(b, c)
    last = cum[Q - 1 : Q, :]
    dy = dy_ref[...].astype(F32)
    step_wide = over_heads(step, heads_ref)
    x_step = x_act * step_wide
    keep = over_heads(jnp.exp(cum) * marks[:, 7:8], heads_ref)
    tail = over_heads(jnp.exp(last - cum) * marks[:, 8:9], heads_ref)
    carry_thin = jnp.broadcast_to(jnp.exp(last) * marks[Q - 1 : Q, 7:8], (8, LANES))
    carry = over_heads(carry_thin, heads_ref)
    state = state_ref[0]
    d_state = held[...]
    d_state_low = d_state.astype(BF16)
    dy_keep = dy * keep
    dy_keep_low = dy_keep.astype(BF16)
    from_state = nn(c, state)
    seen = sum_heads(dy_keep * from_state, heads_ref)
    d_c = nt(dy_keep_low, state)
    to_state = x_step * tail
    d_b = nt(to_state.astype(BF16), d_state_low)
    du_tail = nn(b, d_state_low) * tail
    sent = sum_heads(x_step * du_tail, heads_ref)
    linked = jnp.sum(d_state * state.astype(F32), axis=0, keepdims=True)
    linked = sum_heads(jnp.broadcast_to(linked, (8, MYC)), heads_ref)[0:1, :] * carry_thin[0:1, :]
    held[...] = d_state * carry[0:1, :] + nn(c.T, dy_keep_low)
    lane = lax.broadcasted_iota(jnp.int32, (Q, LANES), 1)
    d_scores = jnp.zeros((Q, Q), F32)
    by_later, by_earlier, du_parts = [], [], []
    for pair in range(MYH // 2):
        cols = slice(pair * LANES, (pair + 1) * LANES)
        steps, dys = x_step[:, cols], dy[:, cols]
        step_both = jnp.concatenate(
            [jnp.where(lane < HD, steps, 0.0), jnp.where(lane < HD, 0.0, steps)], axis=0
        ).astype(BF16)
        dy_both = jnp.concatenate(
            [jnp.where(lane < HD, dys, 0.0), jnp.where(lane < HD, 0.0, dys)], axis=0
        ).astype(BF16)
        met = nt(step_both, dys.astype(BF16))
        mixing = []
        for place, head in enumerate((2 * pair, 2 * pair + 1)):
            decay = jnp.exp(cum_t[head : head + 1, :] - cum[:, head : head + 1] + shut)
            mixing.append((decay * scores).astype(BF16))
            weighed = decay * met[place * Q : (place + 1) * Q, :]
            d_scores = d_scores + weighed
            spent = weighed * scores
            by_later.append(jnp.sum(spent, axis=0, keepdims=True))
            by_earlier.append(jnp.sum(spent, axis=1, keepdims=True))
        du_parts.append(nn(jnp.concatenate(mixing, axis=1), dy_both))
    du = jnp.concatenate(du_parts, axis=1) + du_tail
    d_low = d_scores.astype(BF16)
    d_b = d_b + nn(d_low, c)
    d_c = d_c + nn(d_scores.T.astype(BF16), b)
    dbc_ref[:, :NS] = d_b
    dbc_ref[:, NS:] = d_c
    later = jnp.concatenate(by_later + [jnp.zeros((LANES - MYH, Q), F32)], axis=0).T
    earlier = jnp.zeros((Q, LANES), F32)
    for head in range(MYH):
        earlier = jnp.where(lane == head, by_earlier[head], earlier)
    upper = (at_row <= at_col).astype(F32)
    strict = (at_row > at_col).astype(F32)
    d_log = exact(upper, seen + later - earlier) + exact(strict, sent) + linked
    d_step = sum_heads(x_act * du, heads_ref)
    d_raw = (d_step + rate * d_log) * lax.logistic(shifted)
    live = (lane < MYH).astype(F32)
    d_raw = d_raw * live
    ddt_ref[...] = d_raw.astype(BF16)
    thin_ref[0:1, :] += jnp.sum(d_raw, axis=0, keepdims=True)
    thin_ref[1:2, :] += jnp.sum(d_log * log_decay, axis=0, keepdims=True)
    d_total = (du * step_wide + dy * x_taps[5:6, :]) * slope
    wide_ref[4:5, :] += jnp.sum(d_total, axis=0, keepdims=True)
    wide_ref[5:6, :] += jnp.sum(dy * x_act, axis=0, keepdims=True)
    wide_ref[3:4, :] += jnp.sum(d_total * ext[8 : 8 + Q, :], axis=0, keepdims=True)
    for k in range(KW - 1):
        wide_ref[k : k + 1, :] += jnp.sum(
            d_total * (ext[5 + k : 5 + k + Q, :] * marks[:, 1 + k : 2 + k]), axis=0, keepdims=True
        )
    ext[0:Q, :] = d_total
    ext[Q : Q + 8, :] = ahead[...]
    d_x = d_total * x_taps[3:4, :]
    for k in range(KW - 1):
        d_x = d_x + ext[3 - k : 3 - k + Q, :] * (x_taps[k : k + 1, :] * marks[:, 4 + k : 5 + k])
    ahead[...] = d_total[0:8, :]
    dx_ref[...] = d_x.astype(BF16)


def halo_of(at, blocks):
    return jnp.maximum(at * (Q // 16) - 1, 0)


def run_forward(first, bc_raw, marks, rows, x_taps, bc_taps, head_rows, heads):
    total = first.shape[0]
    blocks = LEN // Q

    def at(s, t):
        return s * blocks + t

    return pl.pallas_call(
        scan_forward,
        grid=(total // LEN, blocks),
        in_specs=[
            pl.BlockSpec((Q, MYC), lambda s, t: (at(s, t), 0)),
            pl.BlockSpec((16, MYC), lambda s, t: (halo_of(at(s, t), blocks), 0)),
            pl.BlockSpec((Q, 2 * NS), lambda s, t: (at(s, t), 0)),
            pl.BlockSpec((16, 2 * NS), lambda s, t: (halo_of(at(s, t), blocks), 0)),
            pl.BlockSpec((Q, LANES), lambda s, t: (at(s, t), MYC // LANES)),
            pl.BlockSpec((Q, 16), lambda s, t: (at(s, t), 0)),
            pl.BlockSpec((1, 1, Q), lambda s, t: (at(s, t), 0, 0)),
            pl.BlockSpec((8, MYC), lambda s, t: (0, 0)),
            pl.BlockSpec((8, 2 * NS), lambda s, t: (0, 0)),
            pl.BlockSpec((8, LANES), lambda s, t: (0, 0)),
            pl.BlockSpec((2 * LANES, MYC), lambda s, t: (0, 0)),
        ],
        out_specs=[
            pl.BlockSpec((Q, MYC), lambda s, t: (at(s, t), 0)),
            pl.BlockSpec((1, NS, MYC), lambda s, t: (at(s, t), 0, 0)),
            pl.BlockSpec((Q, 2 * NS), lambda s, t: (at(s, t), 0)),
        ],
        out_shape=[
            jax.ShapeDtypeStruct((total, MYC), F32),
            jax.ShapeDtypeStruct((total // Q, NS, MYC), BF16),
            jax.ShapeDtypeStruct((total, 2 * NS), BF16),
        ],
        scratch_shapes=[pltpu.VMEM((Q + 8, MYC), F32), pltpu.VMEM((NS, MYC), F32)],
        compiler_params=pltpu.CompilerParams(vmem_limit_bytes=40 * 1024 * 1024),
        cost_estimate=pl.CostEstimate(flops=4 * 10**9, bytes_accessed=20 * 10**6, transcendentals=10**7),
        name="scan_forward",
    )(first, first, bc_raw, bc_raw, first, marks, rows, x_taps, bc_taps, head_rows, heads)


def run_backward(first, bc_act, d_ssm, states, marks, rows, x_taps, head_rows, heads):
    total = first.shape[0]
    blocks = LEN // Q

    def at(s, t):
        return s * blocks + (blocks - 1 - t)

    return pl.pallas_call(
        scan_backward,
        grid=(total // LEN, blocks),
        in_specs=[
            pl.BlockSpec((Q, MYC), lambda s, t: (at(s, t), 0)),
            pl.BlockSpec((16, MYC), lambda s, t: (halo_of(at(s, t), blocks), 0)),
            pl.BlockSpec((Q, 2 * NS), lambda s, t: (at(s, t), 0)),
            pl.BlockSpec((Q, LANES), lambda s, t: (at(s, t), MYC // LANES)),
            pl.BlockSpec((Q, MYC), lambda s, t: (at(s, t), 0)),
            pl.BlockSpec((1, NS, MYC), lambda s, t: (at(s, t), 0, 0)),
            pl.BlockSpec((Q, 16), lambda s, t: (at(s, t), 0)),
            pl.BlockSpec((1, 1, Q), lambda s, t: (at(s, t), 0, 0)),
            pl.BlockSpec((8, MYC), lambda s, t: (0, 0)),
            pl.BlockSpec((8, LANES), lambda s, t: (0, 0)),
            pl.BlockSpec((2 * LANES, MYC), lambda s, t: (0, 0)),
        ],
        out_specs=[
            pl.BlockSpec((Q, MYC), lambda s, t: (at(s, t), 0)),
            pl.BlockSpec((Q, 2 * NS), lambda s, t: (at(s, t), 0)),
            pl.BlockSpec((Q, LANES), lambda s, t: (at(s, t), 0)),
            pl.BlockSpec((8, MYC), lambda s, t: (0, 0)),
            pl.BlockSpec((8, LANES), lambda s, t: (0, 0)),
        ],
        out_shape=[
            jax.ShapeDtypeStruct((total, MYC), BF16),
            jax.ShapeDtypeStruct((total, 2 * NS), F32),
            jax.ShapeDtypeStruct((total, LANES), BF16),
            jax.ShapeDtypeStruct((8, MYC), F32),
            jax.ShapeDtypeStruct((8, LANES), F32),
        ],
        scratch_shapes=[
            pltpu.VMEM((Q + 8, MYC), F32),
            pltpu.VMEM((NS, MYC), F32),
            pltpu.VMEM((8, MYC), F32),
        ],
        compiler_params=pltpu.CompilerParams(vmem_limit_bytes=40 * 1024 * 1024),
        cost_estimate=pl.CostEstimate(flops=10 * 10**9, bytes_accessed=25 * 10**6, transcendentals=10**7),
        name="scan_backward",
    )(first, first, bc_act, first, d_ssm, states, marks, rows, x_taps, head_rows, heads)


def lead(value, by):
    if by == 0:
        return value
    pad = [(0, 0)] * value.ndim
    if by > 0:
        pad[1] = (0, by)
        return jnp.pad(value, pad)[:, by:]
    pad[1] = (-by, 0)
    return jnp.pad(value, pad)[:, :by]


def gather_out(out_weight, split, core, side):
    count = lax.axis_size("zy")
    if split[0] == 1:
        whole = lax.all_gather(out_weight, ("zy", "core", "seq"), axis=0, tiled=True)
        mine = pick(pick(split_heads(whole, 0, split), core), side)
        return mine
    held = lax.ppermute(out_weight, ("core", "seq"), DIAGONAL)
    rows = held.shape[0]
    full = ring_gather(held).reshape(2, count // 2, rows, D)
    mine = in_order(pick(full, core), swap(pick(full, 1 - core), "core"), core)
    return jnp.swapaxes(mine, 0, 1).reshape(MYC, D)


def scatter_out(grad, split, core, side):
    count = lax.axis_size("zy")
    if split[0] == 1:
        own = jnp.zeros((2, 2, MYC, D), BF16)
        own = lax.dynamic_update_slice(own, grad.astype(BF16)[None, None], (core, side, 0, 0))
        whole = join_heads(own, 0, split)
        return lax.psum_scatter(
            whole, ("zy", "core", "seq"), scatter_dimension=0, tiled=True
        ).astype(F32)
    rows = DI // (count * PARTS)
    halves = grad.astype(BF16).reshape(count // 2, 2, rows, D)
    other = swap(pick(halves, 1 - core, 1), "core")
    full = in_order(pick(halves, core, 1), other, core).reshape(count, rows, D)
    held = ring_scatter(full)
    return lax.ppermute(held.astype(BF16), ("core", "seq"), DIAGONAL).astype(F32)


def own_slice(whole, size):
    at = (lax.axis_index("zy") * 2 + lax.axis_index("core")) * 2 + lax.axis_index("seq")
    return lax.dynamic_slice_in_dim(whole, at * size, size, 0)


def body(
    tokens,
    segments,
    norm_gain,
    in_weight,
    conv_weight,
    conv_bias,
    dt_bias,
    a_log,
    d_skip,
    gated_gain,
    out_weight,
    cotangent,
):
    count = lax.axis_size("zy")
    core, side = lax.axis_index("core"), lax.axis_index("seq")
    split = head_split(count)
    rows = tokens.shape[1]
    total = PARTS * rows

    first_cols, gate_cols = split_columns(in_weight, split)
    sent = to_group(jnp.concatenate([first_cols, gate_cols], axis=3), core, side)
    sent = sent.reshape(PARTS * in_weight.shape[0], W1 + MYC)
    w_first = ring_gather(sent[:, :W1]).reshape(D, W1)
    w_gate = ring_gather(sent[:, W1:]).reshape(D, MYC)
    w_out = gather_out(out_weight, split, core, side)

    sizes = (norm_gain.shape[0], conv_weight.size, conv_bias.shape[0], gated_gain.shape[0])
    small = jnp.concatenate([norm_gain, conv_weight.reshape(-1), conv_bias, gated_gain])
    small = small_gather(small[None], core, side).reshape(-1, sum(sizes))
    cuts = np.cumsum(sizes)[:-1]
    gain, taps, bias, gated = (v.reshape(-1).astype(F32) for v in jnp.split(small, cuts, axis=1))
    taps = taps.reshape(CONV, KW)

    def mine(vector, dim=0):
        return pick(pick(split_heads(vector, dim, split), core, dim), side, dim)

    gated_mine = mine(gated)
    x_taps = jnp.concatenate(
        [
            mine(taps[:DI]).T,
            mine(bias[:DI])[None],
            jnp.repeat(mine(d_skip), HD)[None],
            jnp.zeros((2, MYC), F32),
        ],
        axis=0,
    )
    bc_taps = jnp.concatenate(
        [taps[DI:].T, bias[DI:][None], jnp.zeros((3, 2 * NS), F32)], axis=0
    )
    head_rows = jnp.concatenate([mine(dt_bias)[None], mine(a_log)[None]], axis=0)
    head_rows = jnp.pad(head_rows, ((0, 6), (0, LANES - MYH)))
    heads = np.kron(np.eye(LANES, MYH, dtype=np.float32), np.ones((1, HD), np.float32))
    heads = jnp.asarray(np.concatenate([heads, heads], axis=0), BF16)

    segs = group_gather(segments[0], core, side).reshape(2, LEN).astype(F32)
    before = [lead(segs, k - KW + 1) == segs for k in range(KW - 1)]
    place = jnp.arange(LEN)[None, :]
    before = [(m & (place >= KW - 1 - k)).astype(F32) for k, m in enumerate(before)]
    after = [lead(m, KW - 1 - k) for k, m in enumerate(before)]
    ends = segs.reshape(2, LEN // Q, Q)[:, :, -1:]
    starts = jnp.concatenate([jnp.full((2, 1, 1), -1.0, F32), ends[:, :-1]], axis=1)
    keep = (segs.reshape(2, LEN // Q, Q) == starts).astype(F32).reshape(2, LEN)
    tail = (segs.reshape(2, LEN // Q, Q) == ends).astype(F32).reshape(2, LEN)
    marks = jnp.stack([segs] + before + after + [keep, tail] + [jnp.zeros_like(segs)] * 7, axis=-1)
    marks = marks.reshape(total, 16)
    seg_rows = segs.reshape(total // Q, 1, Q)

    def whole_tokens(value):
        near = swap(value, "core")
        far = swap(value, "seq")
        both = swap(far, "core")
        return in_order(in_order(value, far, side), in_order(near, both, side), core)

    token_all = whole_tokens(tokens[0])
    cot_all = whole_tokens(cotangent[0]).reshape(total, D)
    x_all = token_all.reshape(total, D).astype(F32)
    inv_one = lax.rsqrt(jnp.mean(x_all * x_all, axis=-1, keepdims=True) + EPS)
    normed = (x_all * inv_one * gain).astype(BF16)

    first = nn(normed, w_first).astype(BF16)
    bc_mine = first[:, W1 - BCW :]
    bc_core = in_order(bc_mine, swap(bc_mine, "core"), core)
    bc_core = jnp.concatenate([bc_core[0], bc_core[1]], axis=1).reshape(2, total // 2, 2 * BCW)
    bc_half = swap(pick(bc_core, core), "seq")
    bc_other = in_order(bc_half, swap(bc_half, "core"), core).reshape(total, 2 * BCW)
    bc_side = in_order(bc_core.reshape(total, 2 * BCW), bc_other, side)
    bc_raw = jnp.concatenate(
        [bc_side[0, :, :BCW], bc_side[1, :, :BCW], bc_side[0, :, BCW:], bc_side[1, :, BCW:]], axis=1
    )

    y, states, bc_act = run_forward(first, bc_raw, marks, seg_rows, x_taps, bc_taps, head_rows, heads)

    gate = nn(normed, w_gate).astype(BF16).astype(F32)
    sig = lax.logistic(gate)
    silu = gate * sig
    joined = y * silu
    d_two = nt(cot_all, w_out)
    sums = jnp.stack(
        [jnp.sum(joined * joined, axis=-1), jnp.sum(joined * gated_mine * d_two, axis=-1)]
    )
    sums = group_sum(sums)
    inv_two = lax.rsqrt(sums[0] / DI + EPS)[:, None]
    mean_two = (sums[1] / DI)[:, None]
    two = (joined * inv_two * gated_mine).astype(BF16)
    d_joined = inv_two * (gated_mine * d_two) - joined * (inv_two * inv_two * inv_two * mean_two)
    d_ssm = (d_joined * silu).astype(BF16)
    d_gate = (d_joined * y * (sig * (1.0 + gate * (1.0 - sig)))).astype(BF16)
    d_gated = jnp.sum(joined * inv_two * d_two, axis=0)

    def tn(a, b):
        return lax.dot_general(a, b, (((0,), (0,)), ((), ())), preferred_element_type=F32)

    d_out = scatter_out(tn(two, cot_all), split, core, side)
    d_w_gate = ring_scatter(tn(normed, d_gate).reshape(count, D // count, MYC))
    branch = nn(two, w_out).astype(BF16).reshape(2, 2, rows, D)
    branch = group_scatter(branch, core, side)
    block_out = (tokens[0].astype(F32) + branch).astype(BF16)[None]

    d_x, d_bc, d_dt, wide, thin = run_backward(
        first, bc_act, d_ssm, states, marks, seg_rows, x_taps, head_rows, heads
    )
    d_bc = d_bc.reshape(total, 2, 2 * BCW)
    d_core = pick(d_bc, core, 1) + swap(pick(d_bc, 1 - core, 1).astype(BF16), "core").astype(F32)
    d_core = d_core.reshape(total, 2, BCW)
    d_act = pick(d_core, side, 1) + swap(pick(d_core, 1 - side, 1).astype(BF16), "seq").astype(F32)
    d_act = d_act.reshape(2, LEN, BCW)
    raw_mine = bc_mine.astype(F32).reshape(2, LEN, BCW)
    my_taps = lax.dynamic_slice_in_dim(bc_taps, (core * 2 + side) * BCW, BCW, 1)
    reads = [lead(raw_mine, k - KW + 1) * before[k][:, :, None] for k in range(KW - 1)] + [raw_mine]
    bc_total = my_taps[4] + sum(reads[k] * my_taps[k] for k in range(KW))
    bc_sig = lax.logistic(bc_total)
    d_total = d_act * (bc_sig * (1.0 + bc_total * (1.0 - bc_sig)))
    d_bc_raw = d_total * my_taps[3]
    for k in range(KW - 1):
        d_bc_raw = d_bc_raw + lead(d_total, KW - 1 - k) * after[k][:, :, None] * my_taps[k]
    bc_grads = jnp.stack([jnp.sum(d_total * reads[k], axis=(0, 1)) for k in range(KW)] + [jnp.sum(d_total, axis=(0, 1))])
    d_last = jnp.concatenate(
        [d_dt[:, : LANES - BCW], d_bc_raw.reshape(total, BCW).astype(BF16)], axis=1
    )
    d_first = jnp.concatenate([d_x, d_last], axis=1)

    d_w_first = ring_scatter(tn(normed, d_first).reshape(count, D // count, W1))
    d_normed = nt(d_first, w_first) + nt(d_gate, w_gate)
    d_normed = group_scatter(d_normed.astype(BF16).reshape(2, 2, rows, D), core, side)
    x = tokens[0].astype(F32)
    inv = lax.rsqrt(jnp.mean(x * x, axis=-1, keepdims=True) + EPS)
    scaled = gain * d_normed
    input_grad = (
        cotangent[0].astype(F32)
        + inv * scaled
        - x * (inv * inv * inv * jnp.mean(x * scaled, axis=-1, keepdims=True))
    )[None]
    d_gain = jnp.sum(x * inv * d_normed, axis=0)

    d_w = jnp.concatenate([d_w_first, d_w_gate], axis=1).astype(BF16)
    d_w = from_group(d_w.reshape(2, 2, D // (count * PARTS), W1 + MYC), core, side).astype(F32)
    in_sh = join_columns(d_w[..., :W1], d_w[..., W1:], split)

    parts = (
        wide[:KW].reshape(-1),
        wide[KW],
        d_gated,
        bc_grads.reshape(-1),
        thin[0, :MYH],
        thin[1, :MYH],
        jnp.sum(wide[KW + 1].reshape(MYH, HD), axis=1),
        d_gain,
    )
    lengths = [p.shape[0] for p in parts]
    packed = jnp.concatenate(parts)
    packed = jnp.pad(packed, (0, -packed.shape[0] % 1024)).reshape(-1, LANES)
    summed = group_gather(zy_sum(packed), core, side).reshape(2, 2, -1)
    pieces = jnp.split(summed, np.cumsum(lengths), axis=2)
    taps_x, bias_x, gain_two, taps_bc, bias_dt, alog, skip, gain_one = pieces[:8]
    taps_x = jnp.swapaxes(taps_x.reshape(2, 2, KW, MYC), 2, 3)
    taps_bc = taps_bc.reshape(PARTS, KW + 1, BCW)
    conv_w = jnp.concatenate(
        [join_heads(taps_x, 0, split), jnp.swapaxes(taps_bc[:, :KW], 1, 2).reshape(2 * NS, KW)], axis=0
    )
    conv_b = jnp.concatenate([join_heads(bias_x, 0, split), taps_bc[:, KW].reshape(2 * NS)])
    return (
        block_out,
        input_grad,
        own_slice(jnp.sum(gain_one, axis=(0, 1)), norm_gain.shape[0]),
        in_sh,
        own_slice(conv_w, conv_bias.shape[0]),
        own_slice(conv_b, conv_bias.shape[0]),
        join_heads(bias_dt, 0, split),
        join_heads(alog, 0, split),
        join_heads(skip, 0, split),
        own_slice(join_heads(gain_two, 0, split), gated_gain.shape[0]),
        d_out,
    )


def solution(mesh):
    fsdp, seq = mesh.shape["fsdp"], mesh.shape["seq"]
    grid = Mesh(mesh.devices.reshape(fsdp // 2, 2, seq), ("zy", "core", "seq"))
    every = ("zy", "core", "seq")
    rows = P(("zy", "core"), "seq", None)
    in_specs = (
        rows,
        P(("zy", "core"), "seq"),
        P(every),
        P(every, None),
        P(every, None),
        P(every),
        P(),
        P(),
        P(),
        P(every),
        P(every, None),
        rows,
    )
    out_specs = (
        rows,
        rows,
        P(every),
        P(every, None),
        P(every, None),
        P(every),
        P(),
        P(),
        P(),
        P(every),
        P(every, None),
    )
    return jax.shard_map(body, mesh=grid, in_specs=in_specs, out_specs=out_specs, check_vma=False)
```

time: 1430 us -> 654 us (0.46)
  waiting for transfers between devices: 703 us -> 188 us
  matrix products: 311 us -> 89.9 us
  blocking collectives: 123 us -> 0 us
  starting transfers between devices: 10.5 us -> 102 us
  Pallas kernels: 0 us -> 69.3 us
  other arithmetic: 131 us -> 66.4 us
  local copies, waits for them, and re-layouts: 120 us -> 102 us
    reduce_scatter x2 -> x0, waiting for transfers between devices: 581 us -> none  [the longest x1 371 us: body(): lax.psum_scatter(d_in_w, ('fsdp', 'seq'), scatter_dimension=0, tiled=True)]
    dot_general x36 -> x9, matrix products: 311 us -> 89.9 us  [the longest x3 32.3 us: nt(): lax.dot_general(a, b, (((1,), (1,)), ((), ())), preferred_element_type=F32)]
    ppermute x3 -> x85, waiting for transfers between devices: 1.47 us -> 188 us  [the longest x29 77.4 us: swap(): return lax.ppermute(value, axis, SWAP)]
    ppermute x3 -> x85, starting transfers between devices: 10.2 us -> 102 us  [the longest x29 27.3 us: swap(): return lax.ppermute(value, axis, SWAP)]
    unnamed x8 -> x0, waiting for transfers between devices: 78.2 us -> none
    all_gather x3 -> x0, blocking collectives: 76.7 us -> none  [the longest x1 67.8 us: body(): lax.all_gather(conv_weight, ('fsdp', 'seq'), axis=0, tiled=True)]
    pallas_call x0 -> x2, Pallas kernels: none -> 69.3 us  [the longest x1 49.6 us: run_backward(): pl.pallas_call(scan_backward, grid=(total // LEN, blocks), in_specs=[pl.B...]
    unnamed x2 -> x0, blocking collectives: 46 us -> none
  transfers between devices with their start and end apart: 10 -> 85, of which waited for: 7 -> 49; matrix products, arithmetic and copies ran while one was open for 14% -> 27% of each run, Pallas kernels for 0% -> 0%
where the time goes in v1:
time: 654 us; the launch traced here: 644 us
  waiting for transfers between devices  188 us (29%)
  local copies, waits for them, and re-layouts  102 us (16%)
  starting transfers between devices  102 us (16%)
  matrix products  89.9 us (14%)
  Pallas kernels  69.3 us (11%)
  other arithmetic  66.4 us (10%)
  between operations  25.8 us (4%)
    ppermute x29, waiting for transfers between devices, swap(): return lax.ppermute(value, axis, SWAP)  77.4 us
    pallas_call x1, Pallas kernels, run_backward(): pl.pallas_call(scan_backward, grid=(total // LEN, blocks), in_specs=[pl.B...  49.6 us
    dot_general x3, matrix products, nt(): lax.dot_general(a, b, (((1,), (1,)), ((), ())), preferred_element_type=F32)  32.3 us
    dot_general x3, matrix products, nn(): lax.dot_general(a, b, (((1,), (0,)), ((), ())), preferred_element_type=F32)  32 us
    ppermute x9, waiting for transfers between devices, ring_gather(): back = lax.ppermute(back, 'zy', left)  30.3 us
    ppermute x29, starting transfers between devices, swap(): return lax.ppermute(value, axis, SWAP)  27.3 us
    dot_general x3, matrix products, tn(): lax.dot_general(a, b, (((0,), (0,)), ((), ())), preferred_element_type=F32)  25.6 us
    ppermute x9, waiting for transfers between devices, ring_scatter(): ahead = lax.ppermute(one.astype(BF16), 'zy', right)  24.5 us
  transfers between devices with their start and end apart: 85, of which 49 were waited for; matrix products, arithmetic and copies ran while one was open for 27% of the time, Pallas kernels for 0%

profile of v1, /device:TPU:0, one launch (start us, length us, event | category | flops | bytes accessed | tf_op | source)
XLA Modules:
  0.0 643.9 jit_solution(3261447121326655034)
XLA Ops:
  74.5 5.2 collective-permute-done.35
  83.8 5.1 collective-permute-done.9
  92.2 4.7 collective-permute-done.38
  99.6 4.5 collective-permute-done.24
  107.8 4.8 collective-permute-done.11
  116.0 5.5 collective-permute-done.40
  134.1 4.9 collective-permute-done.42
  141.4 6.2 collective-permute-done.13
  161.1 16.4 %collective-permute-done.31 = bf16[512,1536]{1,0:T(8,128)(2,1)S(1)} collective-permute-done((bf16[512,1536]{1,0:T(8,128)(2,1)}, bf16[512,1536]{1,0:T(8,128)(2,1)S(1)}, u32[]{:S(2)}, u32[]{:S(2)}) %collective-permute-start.31) | collective-permute-done | bytes 1572896 | tf_op jit(solution)/shard_map/ppermute | solution.py:37
  210.1 8.9 %convolution_convert_fusion.1.x_ref.x_halo.dt_ref = bf16[2048,896]{1,0:T(8,128)(2,1)S(1)} fusion(bf16[2048,1536]{1,0:T(8,128)(2,1)} %bitcast.568, bf16[1536,896]{1,0:T(8,128)(2,1)S(1)} %bitcast.606), kind=kOutput, calls=%fused_computation.31 | convolution fusion | flops 5638979584 | bytes 12713984 | tf_op jit(solution)/shard_map/dot_general | solution.py:230
  225.1 9.7 %fusion.112 = f32[2048,768]{1,0:T(8,128)} fusion(bf16[2048,1536]{1,0:T(8,128)(2,1)} %bitcast.572, bf16[768,1536]{1,0:T(8,128)(2,1)S(1)} %bitcast.611), kind=kOutput, calls=%fused_computation.357 | convolution fusion | flops 4831838208 | bytes 14942208 | tf_op jit(solution)/shard_map/dot_general | solution.py:226
  237.7 19.7 %scan_forward.1 = (f32[2048,768]{1,0:T(8,128)}, bf16[16,128,768]{2,1,0:T(8,128)(2,1)S(1)}, bf16[2048,256]{1,0:T(8,128)(2,1)S(1)}) custom-call(bf16[2048,896]{1,0:T(8,128)(2,1)S(1)} %convolution_convert_fusion.1.x_ref.x_halo.dt_ref, bf16[2048,896]{1,0:T(8,128)(2,1)S(1)} %convolution_convert_fusion.1.x_ref.x_halo.dt_ref, ...), custom_call_target="tpu_custom_call" | custom-call | flops 4000000000 | bytes 20000000 | tf_op jit(solution)/shard_map/scan_forward/pallas_call | solution.py:450
  257.4 12.1 %multiply_reduce_fusion.3 = (f32[2048]{0:T(1024)S(1)}, f32[2048]{0:T(1024)S(1)}, bf16[2048,768]{1,0:T(8,128)(2,1)}) fusion(f32[2048,768]{1,0:T(8,128)} %get-tuple-element.19, f32[2048,768]{1,0:T(8,128)} %fusion.112, f32[768]{0:T(1024)S(1)} %fusion.89, bf16[2048,1536]{1,0:T(8,128)(2,1)S(1)} %bitcast.571, bf16[1536,768]{1,0:T(8,128)(2,1)S(1)} %bitcast.614), kind=kOutput, calls=%fused_computation.22 | convolution fusion | flops 4850708480 | bytes 24398848 | tf_op jit(solution)/shard_map/dot_general | solution.py:230
  270.4 9.8 %copy.204 = f32[2048,1536]{0,1:T(8,128)} copy(bf16[2048,1536]{1,0:T(8,128)(2,1)} %bitcast.555) | data formatting | bytes 18874368 | tf_op jit(solution)/shard_map/convert_element_type | solution.py:653
  280.7 8.4 %multiply_convert_fusion = bf16[2048,1536]{0,1:T(8,128)(2,1)} fusion(f32[2048,1536]{0,1:T(8,128)} %copy.204, f32[1536]{0:T(1024)S(1)} %reshape.620, f32[2048]{0:T(1024)S(1)} %bitcast.647), kind=kLoop, calls=%fused_computation | loop fusion | flops 9437184 | bytes 18888704 | tf_op jit(solution)/shard_map/convert_element_type | solution.py:655
  289.2 11.8 %convolution_convert_fusion.2 = bf16[768,1536]{1,0:T(8,128)(2,1)S(1)} fusion(bf16[2048,1536]{1,0:T(8,128)(2,1)} %bitcast.573, f32[2048]{0:T(1024)S(1)} %bitcast.631, f32[768]{0:T(1024)S(1)} %fusion.89, f32[2048,768]{1,0:T(8,128)} %get-tuple-element.19, bf16[2048,768]{1,0:T(8,128)(2,1)} %get-tuple-element.126), kind=kOutput, calls=%fused_computation.32 | convolution fusion | flops 4847173632 | bytes 18099200 | tf_op jit(solution)/shard_map/dot_general | solution.py:688
  301.0 10.9 %convolution_convert_fusion = bf16[2048,1536]{1,0:T(8,128)(2,1)} fusion(bf16[768,1536]{1,0:T(8,128)(2,1)S(1)} %bitcast.612, f32[2048]{0:T(1024)S(1)} %bitcast.632, f32[768]{0:T(1024)S(1)} %fusion.89, f32[2048,768]{1,0:T(8,128)} %get-tuple-element.19, bf16[2048,768]{1,0:T(8,128)(2,1)S(1)} %copy-done.23), kind=kOutput, calls=%fused_computation.7 | convolution fusion | flops 4849139712 | bytes 18099200 | tf_op jit(solution)/shard_map/dot_general | solution.py:230
  313.1 7.5 %multiply_convert_fusion.2 = (bf16[2048,768]{1,0:T(8,128)(2,1)S(1)}, bf16[2048,768]{1,0:T(8,128)(2,1)}, f32[768]{0:T(1024)S(1)}) fusion(f32[2048]{0:T(1024)S(1)} %fusion.85, f32[2048,768]{1,0:T(8,128)S(1)} %bitcast.590, f32[2048]{0:T(1024)S(1)} %bitcast.634, f32[768]{0:T(1024)S(1)} %fusion.89, bf16[2048,768]{1,0:T(8,128)(2,1)} %get-tuple-element.126, ...), kind=kLoop, calls=%fused_computation.18 | loop fusion | flops 34602240 | bytes 22042624 | tf_op jit(solution)/shard_map/convert_element_type | solution.py:683
  320.6 49.6 %scan_backward.1 = (bf16[2048,768]{1,0:T(8,128)(2,1)S(1)}, f32[2048,256]{1,0:T(8,128)S(1)}, bf16[2048,128]{1,0:T(8,128)(2,1)S(1)}, f32[8,768]{1,0:T(8,128)S(1)}, f32[8,128]{1,0:T(8,128)S(1)}) custom-call(bf16[2048,896]{1,0:T(8,128)(2,1)} %copy-done, bf16[2048,896]{1,0:T(8,128)(2,1)} %copy-done, bf16[2048,256]{1,0:T(8,128)(2,1)S(1)} %copy-done.8, ...), custom_call_target="tpu_custom_call" | custom-call | flops 10000000000 | bytes 25000000 | tf_op jit(solution)/shard_map/scan_backward/pallas_call | solution.py:490
  379.5 10.3 %fusion.113 = f32[2048,1536]{1,0:T(8,128)} fusion(bf16[2048,768]{1,0:T(8,128)(2,1)} %get-tuple-element.45, bf16[1536,768]{1,0:T(8,128)(2,1)} %bitcast.613), kind=kOutput, calls=%fused_computation.358 | convolution fusion | flops 4831838208 | bytes 18087936 | tf_op jit(solution)/shard_map/dot_general | solution.py:226
  389.8 5.2 fusion.16
  406.6 5.1 collective-permute-done.66
  428.6 6.8 %fusion.106 = (f32[64]{0:T(128)S(1)}, f32[64]{0:T(128)S(1)}, f32[64]{0:T(128)S(1)}, f32[64]{0:T(128)S(1)}, f32[64]{0:T(128)S(1)}, /*index=5*/f32[2,1024,64]{2,1,0:T(8,128)S(1)}) fusion(bf16[2048,896]{1,0:T(8,128)(2,1)} %copy-done, f32[2,1024]{1,0:T(2,128)S(1)} %copy-done.34, f32[2,1024,64]{2,1,0:T(8,128)} %get-tuple-element.63, ...), kind=kLoop, calls=%fused_computation.351 | loop fusion | flops 4193984 | bytes 1862144 | tf_op jit(solution)/shard_map/reduce_sum | solution.py:713
  436.6 12.3 %add_convert_fusion = bf16[2048,1536]{1,0:T(8,128)(2,1)} fusion(f32[2048,1536]{1,0:T(8,128)} %fusion.113, bf16[1536,896]{1,0:T(8,128)(2,1)} %bitcast.605, bf16[2048,64]{1,0:T(8,128)(2,1)S(1)} %bitcast.621, bf16[2048,64]{1,0:T(8,128)(2,1)S(1)} %bitcast.553, bf16[2048,768]{1,0:T(8,128)(2,1)S(1)} %copy-done.10), kind=kOutput, calls=%fused_computation.1 | convolution fusion | flops 5654446080 | bytes 25296896 | tf_op jit(solution)/shard_map/dot_general | solution.py:226
  449.0 8.6 %fusion.7 = f32[8,192,896]{2,1,0:T(8,128)} fusion(bf16[8,192,2048]{2,1,0:T(8,128)(2,1)S(1)} %bitcast.588, bf16[2048,64]{1,0:T(8,128)(2,1)S(1)} %bitcast.622, bf16[2048,64]{1,0:T(8,128)(2,1)S(1)} %bitcast.554, bf16[2048,768]{1,0:T(8,128)(2,1)S(1)} %copy-done.10), kind=kOutput, calls=%fused_computation.29 | convolution fusion | flops 5648154624 | bytes 15466496 | tf_op jit(solution)/shard_map/dot_general | solution.py:688
  477.9 6.4 collective-permute-done.58
  524.5 8.1 %collective-permute-done.64 = bf16[192,896]{1,0:T(8,128)(2,1)S(1)} collective-permute-done((bf16[192,896]{1,0:T(8,128)(2,1)S(1)}, bf16[192,896]{1,0:T(8,128)(2,1)S(1)}, u32[]{:S(2)}, u32[]{:S(2)}) %collective-permute-start.64) | collective-permute-done | bytes 344096 | tf_op jit(solution)/shard_map/ppermute | solution.py:124
  546.1 5.7 collective-permute-start.51
  557.5 6.6 %convert_add_fusion.1 = f32[2,512,1536]{2,1,0:T(8,128)} fusion(bf16[2,512,1536]{2,1,0:T(8,128)(2,1)} %collective-permute-done.46, bf16[2,2,512,1536]{3,2,1,0:T(8,128)(2,1)} %bitcast.575, s32[]{:T(128)S(6)} %select_n.690), kind=kLoop, calls=%fused_computation.16 | loop fusion | flops 4718592 | bytes 12582916 | tf_op jit(solution)/shard_map/add | solution.py:61
  564.1 22.7 %collective-permute-done.51 = bf16[512,1536]{1,0:T(8,128)(2,1)} collective-permute-done((bf16[512,1536]{1,0:T(8,128)(2,1)}, bf16[512,1536]{1,0:T(8,128)(2,1)}, u32[]{:S(2)}, u32[]{:S(2)}) %collective-permute-start.51) | collective-permute-done | bytes 1572896 | tf_op jit(solution)/shard_map/ppermute | solution.py:37
  604.0 25.0 %collective-permute-done.47 = bf16[512,1536]{1,0:T(8,128)(2,1)S(1)} collective-permute-done((bf16[512,1536]{1,0:T(8,128)(2,1)S(1)}, bf16[512,1536]{1,0:T(8,128)(2,1)S(1)}, u32[]{:S(2)}, u32[]{:S(2)}) %collective-permute-start.47) | collective-permute-done | bytes 1572896 | tf_op jit(solution)/shard_map/ppermute | solution.py:37
  629.0 7.3 %fusion.13 = (f32[1,512,1536]{2,1,0:T(8,128)}, bf16[1,512,1536]{2,1,0:T(8,128)(2,1)}) fusion(f32[512]{0:T(512)S(1)} %fusion.91, f32[1536]{0:T(1024)S(1)} %reshape.620, f32[512]{0:T(512)S(1)} %copy-done.46, bf16[512,1536]{1,0:T(8,128)(2,1)} %collective-permute-done.51, f32[2,512,1536]{2,1,0:T(8,128)} %copy-done.12, s32[]{:T(128)S(6)} %select_n.688, ...), kind=kLoop, calls=%fused_computation.38 | loop fusion | flops 10223616 | bytes 17311748 | tf_op jit(solution)/shard_map/broadcast_in_dim | solution.py:725
  (663 shorter events, 281.9 us)
Async XLA Ops:
  0.7 158.1 %collective-permute-start.1 = (bf16[512,1536]{1,0:T(8,128)(2,1)}, bf16[512,1536]{1,0:T(8,128)(2,1)}, u32[]{:S(2)}, u32[]{:S(2)}) collective-permute-start(bf16[512,1536]{1,0:T(8,128)(2,1)} %bitcast.558), channel_id=1, source_target_pairs={{0,2},{2,0},{1,3},{3,1},{4,6},{6,4},{5,7},{7,5},{8,10},{10,8},{9,1... | collective-permute-start | bytes 4718600 | tf_op jit(solution)/shard_map/ppermute | solution.py:37
  1.2 176.8 %collective-permute-start = (bf16[512,1536]{1,0:T(8,128)(2,1)}, bf16[512,1536]{1,0:T(8,128)(2,1)}, u32[]{:S(2)}, u32[]{:S(2)}) collective-permute-start(bf16[512,1536]{1,0:T(8,128)(2,1)} %bitcast.559), channel_id=1, source_target_pairs={{0,1},{1,0},{2,3},{3,2},{4,5},{5,4},{6,7},{7,6},{8,9},{9,8},{10,11... | collective-permute-start | bytes 4718600 | tf_op jit(solution)/shard_map/ppermute | solution.py:37
  8.3 64.5 %collective-permute-start.8 = (bf16[2,48,1664]{2,1,0:T(8,128)(2,1)}, bf16[2,48,1664]{2,1,0:T(8,128)(2,1)}, u32[]{:S(2)}, u32[]{:S(2)}) collective-permute-start(bf16[2,48,1664]{2,1,0:T(8,128)(2,1)} %get-tuple-element.85), channel_id=1, source_target_pairs={{0,2},{2,0},{1,3},{3,1},{4,6},{6,4},{5,7},{7,5},{8,10},{10,8},{9,1... | collective-permute-start | bytes 958472 | tf_op jit(solution)/shard_map/ppermute | solution.py:37
  8.5 61.5 %collective-permute-start.34 = (bf16[96,1536]{1,0:T(8,128)(2,1)}, bf16[96,1536]{1,0:T(8,128)(2,1)}, u32[]{:S(2)}, u32[]{:S(2)}) collective-permute-start(bf16[96,1536]{1,0:T(8,128)(2,1)} %param.35), channel_id=1, source_target_pairs={{0,0},{1,2},{2,1},{3,3},{4,4},{5,6},{6,5},{7,7},{8,8},{9,10},{10,9... | collective-permute-start | bytes 884744 | tf_op jit(solution)/shard_map/ppermute | solution.py:548
  12.6 32.5 %collective-permute-start.3 = (bf16[1,664]{1,0:T(2,128)(2,1)S(1)}, bf16[1,664]{1,0:T(2,128)(2,1)S(1)}, u32[]{:S(2)}, u32[]{:S(2)}) collective-permute-start(bf16[1,664]{1,0:T(2,128)(2,1)S(1)} %broadcast_in_dim.326), channel_id=1, source_target_pairs={{0,1},{1,0},{2,3},{3,2},{4,5},{5,4},{6,7},{7,6},{8,9},{9,8},{10,11... | collective-permute-start | bytes 3992 | tf_op jit(solution)/shard_map/ppermute | solution.py:37
  64.0 91.2 %collective-permute-start.32 = (bf16[512,1536]{1,0:T(8,128)(2,1)}, bf16[512,1536]{1,0:T(8,128)(2,1)}, u32[]{:S(2)}, u32[]{:S(2)}) collective-permute-start(bf16[512,1536]{1,0:T(8,128)(2,1)} %bitcast.99), channel_id=1, source_target_pairs={{0,2},{2,0},{1,3},{3,1},{4,6},{6,4},{5,7},{7,5},{8,10},{10,8},{9,1... | collective-permute-start | bytes 4718600 | tf_op jit(solution)/shard_map/ppermute | solution.py:37
  123.2 17.2 %collective-permute-start.12 = (bf16[192,896]{1,0:T(8,128)(2,1)S(1)}, bf16[192,896]{1,0:T(8,128)(2,1)S(1)}, u32[]{:S(2)}, u32[]{:S(2)}) collective-permute-start(bf16[192,896]{1,0:T(8,128)(2,1)S(1)} %collective-permute-done.10), channel_id=1, source_target_pairs={{0,8},{8,16},{16,24},{24,28},{28,20},{20,12},{12,4},{4,0},{1,9},{9... | collective-permute-start | bytes 1032200 | tf_op jit(solution)/shard_map/ppermute | solution.py:94
  150.5 27.1 %collective-permute-start.31 = (bf16[512,1536]{1,0:T(8,128)(2,1)}, bf16[512,1536]{1,0:T(8,128)(2,1)S(1)}, u32[]{:S(2)}, u32[]{:S(2)}) collective-permute-start(bf16[512,1536]{1,0:T(8,128)(2,1)} %bitcast.99), channel_id=1, source_target_pairs={{0,1},{1,0},{2,3},{3,2},{4,5},{5,4},{6,7},{7,6},{8,9},{9,8},{10,11... | collective-permute-start | bytes 4718600 | tf_op jit(solution)/shard_map/ppermute | solution.py:37
  154.4 45.8 %collective-permute-start.43 = (bf16[4,96,1536]{2,1,0:T(8,128)(2,1)S(1)}, bf16[4,96,1536]{2,1,0:T(8,128)(2,1)}, u32[]{:S(2)}, u32[]{:S(2)}) collective-permute-start(bf16[4,96,1536]{2,1,0:T(8,128)(2,1)S(1)} %dynamic-slice_bitcast_fusion.3), channel_id=1, source_target_pairs={{0,2},{2,0},{1,3},{3,1},{4,6},{6,4},{5,7},{7,5},{8,10},{10,8},{9,1... | collective-permute-start | bytes 3538952 | tf_op jit(solution)/shard_map/ppermute | solution.py:37
  155.1 33.0 %collective-permute-start.14 = (bf16[192,896]{1,0:T(8,128)(2,1)S(1)}, bf16[192,896]{1,0:T(8,128)(2,1)}, u32[]{:S(2)}, u32[]{:S(2)}) collective-permute-start(bf16[192,896]{1,0:T(8,128)(2,1)S(1)} %collective-permute-done.12), channel_id=1, source_target_pairs={{0,8},{8,16},{16,24},{24,28},{28,20},{20,12},{12,4},{4,0},{1,9},{9... | collective-permute-start | bytes 1032200 | tf_op jit(solution)/shard_map/ppermute | solution.py:94
  158.7 30.6 %collective-permute-start.15 = (bf16[192,896]{1,0:T(8,128)(2,1)}, bf16[192,896]{1,0:T(8,128)(2,1)}, u32[]{:S(2)}, u32[]{:S(2)}) collective-permute-start(bf16[192,896]{1,0:T(8,128)(2,1)} %collective-permute-done.13), channel_id=1, source_target_pairs={{8,0},{16,8},{24,16},{28,24},{20,28},{12,20},{4,12},{0,4},{9,1},{1... | collective-permute-start | bytes 1032200 | tf_op jit(solution)/shard_map/ppermute | solution.py:95
  177.5 15.2 %collective-permute-start.29 = (bf16[96,768]{1,0:T(8,128)(2,1)}, bf16[96,768]{1,0:T(8,128)(2,1)}, u32[]{:S(2)}, u32[]{:S(2)}) collective-permute-start(bf16[96,768]{1,0:T(8,128)(2,1)} %slice.367), channel_id=1, source_target_pairs={{0,8},{8,16},{16,24},{24,28},{28,20},{20,12},{12,4},{4,0},{1,9},{9... | collective-permute-start | bytes 442376 | tf_op jit(solution)/shard_map/ppermute | solution.py:98
  178.0 16.0 %collective-permute-start.30 = (bf16[96,768]{1,0:T(8,128)(2,1)}, bf16[96,768]{1,0:T(8,128)(2,1)}, u32[]{:S(2)}, u32[]{:S(2)}) collective-permute-start(bf16[96,768]{1,0:T(8,128)(2,1)} %slice.368), channel_id=1, source_target_pairs={{8,0},{16,8},{24,16},{28,24},{20,28},{12,20},{4,12},{0,4},{9,1},{1... | collective-permute-start | bytes 442376 | tf_op jit(solution)/shard_map/ppermute | solution.py:99
  188.2 14.3 %collective-permute-start.2 = (bf16[512,1536]{1,0:T(8,128)(2,1)}, bf16[512,1536]{1,0:T(8,128)(2,1)S(1)}, u32[]{:S(2)}, u32[]{:S(2)}) collective-permute-start(bf16[512,1536]{1,0:T(8,128)(2,1)} %collective-permute-done), channel_id=1, source_target_pairs={{0,2},{2,0},{1,3},{3,1},{4,6},{6,4},{5,7},{7,5},{8,10},{10,8},{9,1... | collective-permute-start | bytes 4718600 | tf_op jit(solution)/shard_map/ppermute | solution.py:37
  189.3 13.2 %collective-permute-start.33 = (bf16[512,1536]{1,0:T(8,128)(2,1)S(1)}, bf16[512,1536]{1,0:T(8,128)(2,1)S(1)}, u32[]{:S(2)}, u32[]{:S(2)}) collective-permute-start(bf16[512,1536]{1,0:T(8,128)(2,1)S(1)} %collective-permute-done.31), channel_id=1, source_target_pairs={{0,2},{2,0},{1,3},{3,1},{4,6},{6,4},{5,7},{7,5},{8,10},{10,8},{9,1... | collective-permute-start | bytes 4718600 | tf_op jit(solution)/shard_map/ppermute | solution.py:37
  379.4 34.6 %collective-permute-start.48 = (bf16[2048,128]{1,0:T(8,128)(2,1)S(1)}, bf16[2048,128]{1,0:T(8,128)(2,1)S(1)}, u32[]{:S(2)}, u32[]{:S(2)}) collective-permute-start(bf16[2048,128]{1,0:T(8,128)(2,1)S(1)} %convert_bitcast_fusion), channel_id=1, source_target_pairs={{0,2},{2,0},{1,3},{3,1},{4,6},{6,4},{5,7},{7,5},{8,10},{10,8},{9,1... | collective-permute-start | bytes 1572872 | tf_op jit(solution)/shard_map/ppermute | solution.py:37
  406.0 14.8 %collective-permute-start.70 = (bf16[192,768]{1,0:T(8,128)(2,1)}, bf16[192,768]{1,0:T(8,128)(2,1)}, u32[]{:S(2)}, u32[]{:S(2)}) collective-permute-start(bf16[192,768]{1,0:T(8,128)(2,1)} %pad_maximum_fusion.8), channel_id=1, source_target_pairs={{8,0},{16,8},{24,16},{28,24},{20,28},{12,20},{4,12},{0,4},{9,1},{1... | collective-permute-start | bytes 884744 | tf_op jit(solution)/shard_map/ppermute | solution.py:124
  419.0 47.4 %collective-permute-start.75 = (bf16[4,96,1536]{2,1,0:T(8,128)(2,1)}, bf16[4,96,1536]{2,1,0:T(8,128)(2,1)}, u32[]{:S(2)}, u32[]{:S(2)}) collective-permute-start(bf16[4,96,1536]{2,1,0:T(8,128)(2,1)} %dynamic-slice_bitcast_fusion.2), channel_id=1, source_target_pairs={{0,2},{2,0},{1,3},{3,1},{4,6},{6,4},{5,7},{7,5},{8,10},{10,8},{9,1... | collective-permute-start | bytes 3538952 | tf_op jit(solution)/shard_map/ppermute | solution.py:37
  420.4 137.1 %collective-permute-start.46 = (bf16[2,512,1536]{2,1,0:T(8,128)(2,1)}, bf16[2,512,1536]{2,1,0:T(8,128)(2,1)}, u32[]{:S(2)}, u32[]{:S(2)}) collective-permute-start(bf16[2,512,1536]{2,1,0:T(8,128)(2,1)} %dynamic-slice_bitcast_fusion.1), channel_id=1, source_target_pairs={{0,2},{2,0},{1,3},{3,1},{4,6},{6,4},{5,7},{7,5},{8,10},{10,8},{9,1... | collective-permute-start | bytes 9437192 | tf_op jit(solution)/shard_map/ppermute | solution.py:37
  423.2 68.9 %collective-permute-start.71 = (bf16[192,768]{1,0:T(8,128)(2,1)}, bf16[192,768]{1,0:T(8,128)(2,1)}, u32[]{:S(2)}, u32[]{:S(2)}) collective-permute-start(bf16[192,768]{1,0:T(8,128)(2,1)} %get-tuple-element.56), channel_id=1, source_target_pairs={{8,0},{16,8},{24,16},{28,24},{20,28},{12,20},{4,12},{0,4},{9,1},{1... | collective-permute-start | bytes 884744 | tf_op jit(solution)/shard_map/ppermute | solution.py:124
  470.2 23.9 %collective-permute-start.62 = (bf16[192,896]{1,0:T(8,128)(2,1)S(1)}, bf16[192,896]{1,0:T(8,128)(2,1)S(1)}, u32[]{:S(2)}, u32[]{:S(2)}) collective-permute-start(bf16[192,896]{1,0:T(8,128)(2,1)S(1)} %pad_maximum_fusion.6), channel_id=1, source_target_pairs={{8,0},{16,8},{24,16},{28,24},{20,28},{12,20},{4,12},{0,4},{9,1},{1... | collective-permute-start | bytes 1032200 | tf_op jit(solution)/shard_map/ppermute | solution.py:124
  476.2 14.4 %collective-permute-start.77 = (bf16[96,1536]{1,0:T(8,128)(2,1)S(1)}, bf16[96,1536]{1,0:T(8,128)(2,1)S(1)}, u32[]{:S(2)}, u32[]{:S(2)}) collective-permute-start(bf16[96,1536]{1,0:T(8,128)(2,1)S(1)} %pad_maximum_fusion.9), channel_id=1, source_target_pairs={{0,8},{8,16},{16,24},{24,28},{28,20},{20,12},{12,4},{4,0},{1,9},{9... | collective-permute-start | bytes 884744 | tf_op jit(solution)/shard_map/ppermute | solution.py:123
  484.4 13.6 %collective-permute-start.59 = (bf16[192,896]{1,0:T(8,128)(2,1)S(1)}, bf16[192,896]{1,0:T(8,128)(2,1)S(1)}, u32[]{:S(2)}, u32[]{:S(2)}) collective-permute-start(bf16[192,896]{1,0:T(8,128)(2,1)S(1)} %fusion.37), channel_id=1, source_target_pairs={{0,8},{8,16},{16,24},{24,28},{28,20},{20,12},{12,4},{4,0},{1,9},{9... | collective-permute-start | bytes 1032200 | tf_op jit(solution)/shard_map/ppermute | solution.py:123
  494.1 12.9 %collective-permute-start.68 = (bf16[192,768]{1,0:T(8,128)(2,1)S(1)}, bf16[192,768]{1,0:T(8,128)(2,1)S(1)}, u32[]{:S(2)}, u32[]{:S(2)}) collective-permute-start(bf16[192,768]{1,0:T(8,128)(2,1)S(1)} %copy-done.32), channel_id=1, source_target_pairs={{0,8},{8,16},{16,24},{24,28},{28,20},{20,12},{12,4},{4,0},{1,9},{9... | collective-permute-start | bytes 884744 | tf_op jit(solution)/shard_map/ppermute | solution.py:123
  498.0 45.6 %collective-permute-start.50 = (bf16[2,512,1536]{2,1,0:T(8,128)(2,1)S(1)}, bf16[2,512,1536]{2,1,0:T(8,128)(2,1)S(1)}, u32[]{:S(2)}, u32[]{:S(2)}) collective-permute-start(bf16[2,512,1536]{2,1,0:T(8,128)(2,1)S(1)} %dynamic-slice_bitcast_fusion), channel_id=1, source_target_pairs={{0,2},{2,0},{1,3},{3,1},{4,6},{6,4},{5,7},{7,5},{8,10},{10,8},{9,1... | collective-permute-start | bytes 9437192 | tf_op jit(solution)/shard_map/ppermute | solution.py:37
  507.0 14.4 %collective-permute-start.82 = (bf16[96,1536]{1,0:T(8,128)(2,1)S(1)}, bf16[96,1536]{1,0:T(8,128)(2,1)S(1)}, u32[]{:S(2)}, u32[]{:S(2)}) collective-permute-start(bf16[96,1536]{1,0:T(8,128)(2,1)S(1)} %get-tuple-element.66), channel_id=1, source_target_pairs={{8,0},{16,8},{24,16},{28,24},{20,28},{12,20},{4,12},{0,4},{9,1},{1... | collective-permute-start | bytes 884744 | tf_op jit(solution)/shard_map/ppermute | solution.py:124
  509.3 13.9 %collective-permute-start.60 = (bf16[192,896]{1,0:T(8,128)(2,1)S(1)}, bf16[192,896]{1,0:T(8,128)(2,1)S(1)}, u32[]{:S(2)}, u32[]{:S(2)}) collective-permute-start(bf16[192,896]{1,0:T(8,128)(2,1)S(1)} %get-tuple-element.47), channel_id=1, source_target_pairs={{0,8},{8,16},{16,24},{24,28},{28,20},{20,12},{12,4},{4,0},{1,9},{9... | collective-permute-start | bytes 1032200 | tf_op jit(solution)/shard_map/ppermute | solution.py:123
  515.5 20.0 %collective-permute-start.79 = (bf16[96,1536]{1,0:T(8,128)(2,1)S(1)}, bf16[96,1536]{1,0:T(8,128)(2,1)S(1)}, u32[]{:S(2)}, u32[]{:S(2)}) collective-permute-start(bf16[96,1536]{1,0:T(8,128)(2,1)S(1)} %get-tuple-element.65), channel_id=1, source_target_pairs={{0,8},{8,16},{16,24},{24,28},{28,20},{20,12},{12,4},{4,0},{1,9},{9... | collective-permute-start | bytes 884744 | tf_op jit(solution)/shard_map/ppermute | solution.py:123
  523.1 14.5 %collective-permute-start.83 = (bf16[96,1536]{1,0:T(8,128)(2,1)S(1)}, bf16[96,1536]{1,0:T(8,128)(2,1)S(1)}, u32[]{:S(2)}, u32[]{:S(2)}) collective-permute-start(bf16[96,1536]{1,0:T(8,128)(2,1)S(1)} %fusion.42), channel_id=1, source_target_pairs={{8,0},{16,8},{24,16},{28,24},{20,28},{12,20},{4,12},{0,4},{9,1},{1... | collective-permute-start | bytes 884744 | tf_op jit(solution)/shard_map/ppermute | solution.py:124
  546.1 40.7 %collective-permute-start.51 = (bf16[512,1536]{1,0:T(8,128)(2,1)}, bf16[512,1536]{1,0:T(8,128)(2,1)}, u32[]{:S(2)}, u32[]{:S(2)}) collective-permute-start(bf16[512,1536]{1,0:T(8,128)(2,1)} %fusion.20), channel_id=1, source_target_pairs={{0,1},{1,0},{2,3},{3,2},{4,5},{5,4},{6,7},{7,6},{8,9},{9,8},{10,11... | collective-permute-start | bytes 4718600 | tf_op jit(solution)/shard_map/ppermute | solution.py:37
  593.0 36.0 %collective-permute-start.47 = (bf16[512,1536]{1,0:T(8,128)(2,1)S(1)}, bf16[512,1536]{1,0:T(8,128)(2,1)S(1)}, u32[]{:S(2)}, u32[]{:S(2)}) collective-permute-start(bf16[512,1536]{1,0:T(8,128)(2,1)S(1)} %fusion.19), channel_id=1, source_target_pairs={{0,1},{1,0},{2,3},{3,2},{4,5},{5,4},{6,7},{7,6},{8,9},{9,8},{10,11... | collective-permute-start | bytes 4718600 | tf_op jit(solution)/shard_map/ppermute | solution.py:37
  602.3 34.0 %collective-permute-start.55 = (f32[56,128]{1,0:T(8,128)S(1)}, f32[56,128]{1,0:T(8,128)S(1)}, u32[]{:S(2)}, u32[]{:S(2)}) collective-permute-start(f32[56,128]{1,0:T(8,128)S(1)} %get-tuple-element.42), channel_id=1, source_target_pairs={{0,1},{1,0},{2,3},{3,2},{4,5},{5,4},{6,7},{7,6},{8,9},{9,8},{10,11... | collective-permute-start | bytes 86024 | tf_op jit(solution)/shard_map/ppermute | solution.py:37
  (135 other events, 1437.7 us)

commit v2 on v1

v2 whole, which is shorter than its diff:
```python
import functools

import jax
import jax.numpy as jnp
import numpy as np
from jax import lax
from jax.experimental import pallas as pl
from jax.experimental.pallas import tpu as pltpu
from jax.sharding import Mesh
from jax.sharding import PartitionSpec as P

D = 1536
NH = 48
HD = 64
NS = 128
KW = 4
DI = 3072
CONV = 3328
LEN = 1024

EPS = 1e-05
HIGH = lax.Precision.HIGHEST
F32 = jnp.float32
BF16 = jnp.bfloat16

PARTS = 4
MYH = NH // PARTS
MYC = MYH * HD
LANES = 128
BC = 2 * NS
W1 = MYC + BC + LANES
GROUPS = 2
GH = MYH // GROUPS
GC = GH * HD
Q = 128
FAR = -1e30
VMEM_LIMIT = 56 * 1024 * 1024

SWAP = [(0, 1), (1, 0)]


def swap(value, axis):
    return lax.ppermute(value, axis, SWAP)


def pick(value, at, dim=0):
    return lax.dynamic_index_in_dim(value, at, dim, False)


def in_order(mine, other, place):
    buf = jnp.zeros((2,) + mine.shape, mine.dtype)
    buf = lax.dynamic_update_index_in_dim(buf, mine, place, 0)
    return lax.dynamic_update_index_in_dim(buf, other, 1 - place, 0)


GROUP = ("core", "seq")


def to_peer(value, r):
    return (value, GROUP, [(g, g ^ r) for g in range(PARTS)])


def ring_order(count):
    return list(range(0, count, 2)) + list(range(count - 1, 0, -2))


def ring_pairs(count):
    order = ring_order(count)
    right = [(order[i], order[(i + 1) % count]) for i in range(count)]
    return right, [(b, a) for a, b in right]


def ring_place(count):
    zy = lax.axis_index("zy")
    place = jnp.where(zy % 2 == 0, zy // 2, count - 1 - zy // 2)

    def order(at):
        at = at % count
        return jnp.where(at < count // 2, 2 * at, 2 * (count - at) - 1)

    return place, order


class Task:
    def __init__(self, steps):
        self.steps, self.value, self.done = steps, None, False
        self.moves = next(steps)

    def take(self, arrived):
        try:
            self.moves = self.steps.send(arrived)
        except StopIteration as end:
            self.value, self.done = end.value, True


def stage(tasks, work=None, *args):
    tasks = [t for t in tasks if not t.done]
    values = [[m[0] for m in t.moves] for t in tasks]
    values, args = lax.optimization_barrier((values, args))
    arrived = [
        [lax.ppermute(v, m[1], m[2]) for v, m in zip(vs, t.moves)] for vs, t in zip(values, tasks)
    ]
    result = None if work is None else work(*args)
    if work is None:
        arrived = lax.optimization_barrier(arrived)
    else:
        arrived, result = lax.optimization_barrier((arrived, result))
    for t, got in zip(tasks, arrived):
        t.take(got)
    return result


def finish(tasks):
    while not all(t.done for t in tasks):
        stage(tasks)


def gather_steps(block, cuts):
    count = lax.axis_size("zy")
    rows = block.shape[0]
    half = rows // 2
    right, left = ring_pairs(count)
    place, order = ring_place(count)
    ends = list(cuts[1:]) + [block.shape[1]]
    fulls = [jnp.zeros((count, rows, b - a), block.dtype) for a, b in zip(cuts, ends)]

    def put(part, at, off=0):
        for i, (a, b) in enumerate(zip(cuts, ends)):
            fulls[i] = lax.dynamic_update_slice(fulls[i], part[None, :, a:b], (order(at), off, 0))

    put(block, place)
    ahead = back = block
    for step in range(1, count // 2):
        ahead, back = yield [(ahead, "zy", right), (back, "zy", left)]
        put(ahead, place - step + count)
        put(back, place + step)
    ahead, back = yield [(ahead[:half], "zy", right), (back[half:], "zy", left)]
    put(ahead, place + count // 2)
    put(back, place + count // 2, half)
    return fulls


def scatter_steps(full):
    count, rows, cols = full.shape
    half = rows // 2
    right, left = ring_pairs(count)
    place, order = ring_place(count)

    def get(at, off=0, size=rows):
        return lax.dynamic_slice(full, (order(at), off, 0), (1, size, cols))[0].astype(F32)

    far = place + count // 2
    one, two = get(far, 0, half), get(far, half, rows - half)
    for step in range(count // 2 - 1, -1, -1):
        ahead, back = yield [(one.astype(BF16), "zy", right), (two.astype(BF16), "zy", left)]
        if step == 0:
            break
        one, two = get(place + step), get(place + count - step)
        if step == count // 2 - 1:
            one = jnp.concatenate([one[:half] + ahead, one[half:]], axis=0)
            two = jnp.concatenate([two[:half], two[half:] + back], axis=0)
        else:
            one, two = one + ahead, two + back
    return get(place) + ahead.astype(F32) + back.astype(F32)


def small_steps(value, core, side):
    count = lax.axis_size("zy")
    got = yield [to_peer(value, r) for r in range(1, PARTS)]
    held = jnp.stack([value] + list(got))
    held = held.reshape((2, 2) + value.shape)
    held = jnp.where(core == 0, held, held[::-1])
    held = jnp.where(side == 0, held, held[:, ::-1]).reshape((1, PARTS) + value.shape)
    bit = 1
    while bit < count:
        pairs = [(i, i ^ bit) for i in range(count)]
        (got,) = yield [(held, "zy", pairs)]
        upper = (lax.axis_index("zy") // bit) % 2
        held = jnp.concatenate([jnp.where(upper == 0, held, got), jnp.where(upper == 0, got, held)])
        bit *= 2
    return held


def group_steps(value):
    got = yield [to_peer(value, r) for r in range(1, PARTS)]
    return [value] + list(got)


def token_steps(value, pieces):
    rows = value.shape[0]
    cuts = [16 * (rows // 16 * i // pieces) for i in range(pieces + 1)]
    far, both = [], []
    moves = [(value, "core", SWAP)]
    for i in range(pieces):
        got = yield moves + [(value[cuts[i] : cuts[i + 1]], "seq", SWAP)]
        if i == 0:
            near = got[0]
        else:
            both.append(got[0])
        far.append(got[-1])
        moves = [(got[-1], "core", SWAP)]
    (got,) = yield moves
    return near, far, both + [got]


def peer_steps(blocks):
    got = yield [to_peer(blocks[r], r) for r in range(1, PARTS)]
    return [blocks[0]] + list(got)


def sum_steps(value, pieces):
    (got,) = yield [(value[2:], "core", SWAP)]
    sent = (value[1].astype(F32) + got[1].astype(F32)).astype(BF16)
    rows = sent.shape[0] // pieces
    arrived = []
    for i in range(pieces):
        (far,) = yield [(sent[i * rows : (i + 1) * rows], "seq", SWAP)]
        arrived.append(far)
    return value[0].astype(F32) + got[0].astype(F32) + jnp.concatenate(arrived, axis=0).astype(F32)


def far_steps(value, pieces):
    (got,) = yield [(value[1], "core", SWAP)]
    kept = value[0].astype(F32) + got.astype(F32)
    if not pieces:
        return kept
    sent = kept.astype(BF16)
    rows = sent.shape[0] // pieces
    arrived = []
    for i in range(pieces):
        (got,) = yield [(sent[i * rows : (i + 1) * rows], "seq", SWAP)]
        arrived.append(got)
    return jnp.concatenate(arrived, axis=0)


def small_sum_steps(parts, core, side):
    count = lax.axis_size("zy")
    lengths = [p.shape[0] for p in parts]
    packed = jnp.concatenate(parts)
    packed = jnp.pad(packed, (0, -packed.shape[0] % 1024)).reshape(-1, LANES)
    bit = 1
    while bit < count:
        (got,) = yield [(packed, "zy", [(i, i ^ bit) for i in range(count)])]
        packed = packed + got
        bit *= 2
    (got,) = yield [(packed, "core", SWAP)]
    packed = in_order(packed, got, core)
    (got,) = yield [(packed, "seq", SWAP)]
    packed = jnp.swapaxes(in_order(packed, got, side), 0, 1).reshape(2, 2, -1)
    return jnp.split(packed, np.cumsum(lengths), axis=2)[: len(lengths)]


def zy_exchange(value, bit):
    count = lax.axis_size("zy")
    return lax.ppermute(value, "zy", [(i, i ^ bit) for i in range(count)])


def zy_sum(value):
    count = lax.axis_size("zy")
    bit = 1
    while bit < count:
        value = value + zy_exchange(value, bit)
        bit *= 2
    return value


def head_split(count):
    rows = DI // count
    if rows % (2 * HD) == 0 and count % 2 == 0:
        return count // 2, rows // (2 * HD)
    return 1, MYH


def split_heads(value, dim, split):
    q, i = split
    size = value.shape[dim]
    unit = size // NH
    shape = value.shape
    value = value.reshape(shape[:dim] + (2, q, 2, i * unit) + shape[dim + 1 :])
    value = jnp.swapaxes(value, dim + 1, dim + 2)
    return value.reshape(shape[:dim] + (2, 2, size // PARTS) + shape[dim + 1 :])


def join_heads(value, dim, split):
    q, i = split
    shape = value.shape
    mine = shape[dim + 2]
    value = value.reshape(shape[:dim] + (2, 2, q, mine // q) + shape[dim + 3 :])
    value = jnp.swapaxes(value, dim + 1, dim + 2)
    return value.reshape(shape[:dim] + (PARTS * mine,) + shape[dim + 3 :])


HALF = LANES // 2


def half_places(split, core, side):
    q, i = split
    return [((core * q + at) * 2 + side) * i + k for at in range(q) for k in range(i)]


def halves(tile_of, places):
    tiles = []
    for at in range(0, len(places), 2):
        one, two = places[at], places[at + 1]
        if one % 2 == 0 and two == one + 1:
            tiles.append(tile_of(one // 2))
            continue
        left, right = tile_of(one // 2), tile_of(two // 2)
        left = pltpu.roll(left, HALF, 1) if one % 2 else left
        right = right if two % 2 else pltpu.roll(right, HALF, 1)
        lane = lax.broadcasted_iota(jnp.int32, left.shape, 1)
        tiles.append(jnp.where(lane < HALF, left, right))
    return tiles


def head_choice(split):
    choice = np.zeros((PARTS, NH, LANES), np.float32)
    for g in range(PARTS):
        for lane, head in enumerate(half_places(split, g // 2, g % 2)):
            choice[g, head, lane] = 1.0
    return choice


def split_kernel(split, at_ref, w_ref, choice_ref, out_ref):
    me = at_ref[0]

    def tile_of(base):
        return lambda t: w_ref[:, base + t * LANES : base + (t + 1) * LANES].astype(F32)

    bc = w_ref[:, 2 * DI : 2 * DI + BC]
    steps = w_ref[:, DI + CONV :]
    for g in range(PARTS):
        places = half_places(split, g // 2, g % 2)
        at = me ^ g
        tiles = halves(tile_of(DI), places)
        for k, tile in enumerate(tiles):
            out_ref[at, :, k * LANES : (k + 1) * LANES] = tile.astype(BF16)
        out_ref[at, :, MYC : MYC + BC] = bc
        out_ref[at, :, MYC + BC : W1] = nn(steps, choice_ref[g]).astype(BF16)
        for k, tile in enumerate(halves(tile_of(0), places)):
            out_ref[at, :, W1 + k * LANES : W1 + (k + 1) * LANES] = tile.astype(BF16)


def smem(shape=None):
    return pl.BlockSpec(memory_space=pltpu.SMEM)


def split_columns(weight, split, me):
    return pl.pallas_call(
        functools.partial(split_kernel, split),
        out_shape=jax.ShapeDtypeStruct((PARTS, weight.shape[0], W1 + MYC), BF16),
        in_specs=[smem(), pl.BlockSpec(), pl.BlockSpec()],
        name="split_columns",
    )(me, weight, jnp.asarray(head_choice(split), BF16))


def assemble_kernel(at_ref, one, two, three, four, first_ref, gate_ref):
    me = at_ref[0]
    for r, ref in enumerate((one, two, three, four)):
        first_ref[me ^ r] = ref[:, :W1]
        gate_ref[me ^ r] = ref[:, W1:]


def assemble_rows(blocks, me):
    rows = blocks[0].shape[0]
    first, gate = pl.pallas_call(
        assemble_kernel,
        out_shape=[
            jax.ShapeDtypeStruct((PARTS, rows, W1), BF16),
            jax.ShapeDtypeStruct((PARTS, rows, MYC), BF16),
        ],
        in_specs=[smem()] + [pl.BlockSpec()] * PARTS,
        name="assemble_rows",
    )(me, *blocks)
    return first.reshape(PARTS * rows, W1), gate.reshape(PARTS * rows, MYC)


def hand_back_kernel(at_ref, *refs):
    *ins, out_ref = refs
    me = at_ref[0]
    for g in range(PARTS):
        at = 0
        for ref in ins:
            out_ref[me ^ g, :, at : at + ref.shape[2]] = ref[g].astype(BF16)
            at += ref.shape[2]


def hand_back(blocks, me):
    blocks = [b.reshape(PARTS, -1, b.shape[1]) for b in blocks]
    return pl.pallas_call(
        hand_back_kernel,
        out_shape=jax.ShapeDtypeStruct((PARTS, blocks[0].shape[1], W1 + MYC), BF16),
        in_specs=[smem()] + [pl.BlockSpec()] * len(blocks),
        name="hand_back",
    )(me, *blocks)


def join_kernel(split, at_ref, one, two, three, four, choice_ref, out_ref, by):
    me = at_ref[0]
    for r, ref in enumerate((one, two, three, four)):
        by[me ^ r] = ref[...].astype(F32)
    where = {}
    for g in range(PARTS):
        for at, place in enumerate(half_places(split, g // 2, g % 2)):
            where[place] = (g, at)

    def put(base, column):
        for t in range(DI // LANES):
            tiles = []
            for k in range(2):
                g, at = where[2 * t + k]
                start = column + at // 2 * LANES
                tile = by[g, :, start : start + LANES]
                tiles.append(tile if at % 2 == k else pltpu.roll(tile, HALF, 1))
            lane = lax.broadcasted_iota(jnp.int32, tiles[0].shape, 1)
            out_ref[:, base + t * LANES : base + (t + 1) * LANES] = jnp.where(lane < HALF, tiles[0], tiles[1])

    put(0, W1)
    put(DI, 0)
    out_ref[:, 2 * DI : 2 * DI + BC] = sum(by[g, :, MYC : MYC + BC] for g in range(PARTS))
    out_ref[:, DI + CONV :] = sum(
        nt(by[g, :, MYC + BC : W1].astype(BF16), choice_ref[g]) for g in range(PARTS)
    )


def join_columns(blocks, split, me):
    rows = blocks[0].shape[0]
    return pl.pallas_call(
        functools.partial(join_kernel, split),
        out_shape=jax.ShapeDtypeStruct((rows, 2 * DI + BC + NH), F32),
        in_specs=[smem()] + [pl.BlockSpec()] * (PARTS + 1),
        scratch_shapes=[pltpu.VMEM((PARTS, rows, W1 + MYC), F32)],
        name="join_columns",
    )(me, *blocks, jnp.asarray(head_choice(split), BF16))


DIAGONAL = [(0, 0), (1, 2), (2, 1), (3, 3)]


def nt(a, b):
    return lax.dot_general(a, b, (((1,), (1,)), ((), ())), preferred_element_type=F32)


def nn(a, b):
    return lax.dot_general(a, b, (((1,), (0,)), ((), ())), preferred_element_type=F32)


def exact(a, b):
    return lax.dot_general(
        a, b, (((1,), (0,)), ((), ())), preferred_element_type=F32, precision=HIGH
    )


def in_two(value, axis):
    top = value.astype(BF16)
    return jnp.concatenate([top, (value - top.astype(F32)).astype(BF16)], axis=axis)


def over_heads(value, heads_ref):
    return nn(in_two(value, 1), heads_ref[...])


def sum_heads(value, heads_ref):
    top = value.astype(BF16)
    low = (value - top.astype(F32)).astype(BF16)
    heads = heads_ref[:LANES, :]
    return nt(top, heads) + nt(low, heads)


PIECES = 4
PROJECT = 128


def project_kernel(*refs):
    *sources, gain_ref, w_ref, first_ref, normed_ref, turned_ref, held = refs
    step = pl.program_id(0)
    own, near, far, both = sources[0], sources[1], sources[2 : 2 + PIECES], sources[2 + PIECES :]
    order = [own] * PIECES + list(far) + [near] * PIECES + list(both)
    for ref in sources:
        steps = [i for i, r in enumerate(order) if r is ref]

        @pl.when((step >= steps[0]) & (step <= steps[-1]))
        def _():
            held[...] = ref[...]

    x = held[...].astype(F32)
    inv = lax.rsqrt(jnp.mean(x * x, axis=-1, keepdims=True) + EPS)
    normed = x * inv * gain_ref[...]
    low = normed.astype(BF16)
    normed_ref[...] = low
    first_ref[...] = nn(low, w_ref[...]).astype(BF16)
    turned_ref[...] = normed.T.astype(BF16)


def project(own, near, far, both, gain, w_first):
    rows = own.shape[0]
    steps = rows // PROJECT
    total = PARTS * rows

    def at(start):
        return lambda t: (jnp.clip(t - start, 0, steps - 1), 0)

    still = lambda t: (0, 0)
    return pl.pallas_call(
        project_kernel,
        grid=(total // PROJECT,),
        in_specs=[
            pl.BlockSpec((PROJECT, D), at(0)),
            pl.BlockSpec((PROJECT, D), at(2 * steps)),
        ]
        + [pl.BlockSpec((PROJECT, D), still)] * (2 * PIECES)
        + [pl.BlockSpec((1, D), still), pl.BlockSpec((D, W1), still)],
        out_specs=[
            pl.BlockSpec((PROJECT, W1), lambda t: (t, 0)),
            pl.BlockSpec((PROJECT, D), lambda t: (t, 0)),
            pl.BlockSpec((D, PROJECT), lambda t: (0, t)),
        ],
        out_shape=[
            jax.ShapeDtypeStruct((total, W1), BF16),
            jax.ShapeDtypeStruct((total, D), BF16),
            jax.ShapeDtypeStruct((D, total), BF16),
        ],
        scratch_shapes=[pltpu.VMEM((PROJECT, D), BF16)],
        compiler_params=pltpu.CompilerParams(vmem_limit_bytes=VMEM_LIMIT),
        cost_estimate=pl.CostEstimate(flops=12 * 10**9, bytes_accessed=30 * 10**6, transcendentals=10**4),
        name="project",
    )(own, near, *far, *both, gain, w_first)


def softplus(value):
    return jnp.maximum(value, 0.0) + jnp.log1p(jnp.exp(-jnp.abs(value)))


def conv_total(ext, raw_ref, halo_ref, taps_ref, marks):
    ext[0:8, :] = halo_ref[8:16, :].astype(F32)
    ext[8 : 8 + Q, :] = raw_ref[...].astype(F32)
    total = taps_ref[4:5, :] + ext[8 : 8 + Q, :] * taps_ref[3:4, :]
    for k in range(KW - 1):
        total = total + ext[5 + k : 5 + k + Q, :] * taps_ref[k : k + 1, :] * marks[:, 1 + k : 2 + k]
    return total


def conv_back(d_total, ext, ahead, taps_ref, marks, sums_ref):
    sums_ref[4:5, :] += jnp.sum(d_total, axis=0, keepdims=True)
    sums_ref[3:4, :] += jnp.sum(d_total * ext[8 : 8 + Q, :], axis=0, keepdims=True)
    for k in range(KW - 1):
        sums_ref[k : k + 1, :] += jnp.sum(
            d_total * (ext[5 + k : 5 + k + Q, :] * marks[:, 1 + k : 2 + k]), axis=0, keepdims=True
        )
    ext[0:Q, :] = d_total
    ext[Q : Q + 8, :] = ahead[...]
    d_raw = d_total * taps_ref[3:4, :]
    for k in range(KW - 1):
        d_raw = d_raw + ext[3 - k : 3 - k + Q, :] * (taps_ref[k : k + 1, :] * marks[:, 4 + k : 5 + k])
    ahead[...] = d_total[0:8, :]
    return d_raw


def decays(dt_ref, head_ref, lower):
    raw = dt_ref[...].astype(F32)
    lane = lax.broadcasted_iota(jnp.int32, (Q, LANES), 1)
    live = (lane < MYH).astype(F32)
    shifted = raw * live + head_ref[0:1, :]
    step = softplus(shifted) * live
    rate = -jnp.exp(head_ref[1:2, :])
    log_decay = rate * step
    return shifted, step, rate, log_decay, exact(lower, log_decay)


def scan_forward(
    side_ref, x_ref, x_halo, bc_ref, bc_halo, dt_ref, marks_ref, row_ref, x_taps, bc_taps, head_ref, heads_ref,
    y_ref, state_ref, bc_out, ext, bc_ext, held,
):
    chunk = pl.program_id(1)

    @pl.when(chunk == 0)
    def _():
        held[...] = jnp.zeros_like(held)

    marks = marks_ref[...]
    x_act = conv_total(ext, x_ref, x_halo, x_taps, marks)
    x_act = x_act * lax.logistic(x_act)
    bc_act = conv_total(bc_ext, bc_ref, bc_halo, bc_taps, marks)
    bc_act = (bc_act * lax.logistic(bc_act)).astype(BF16)
    bc_out[...] = bc_act
    b, c = bc_act[:, :NS], bc_act[:, NS:]
    at_row = lax.broadcasted_iota(jnp.int32, (Q, Q), 0)
    at_col = lax.broadcasted_iota(jnp.int32, (Q, Q), 1)
    lower = (at_row >= at_col).astype(F32)
    _, step, _, _, cum = decays(dt_ref, head_ref, lower)
    cum_t = cum.T
    shut = jnp.where((at_row >= at_col) & (marks[:, 0:1] == row_ref[0]), 0.0, FAR)
    scores = nt(c, b)
    state = held[...]
    state_low = state.astype(BF16)
    state_ref[0] = state_low
    last = cum[Q - 1 : Q, :]
    x_step = x_act * over_heads(step, heads_ref)
    keep = over_heads(jnp.exp(cum) * marks[:, 7:8], heads_ref)
    y = nn(c, state_low) * keep + x_act * x_taps[5:6, :]
    tail = over_heads(jnp.exp(last - cum) * marks[:, 8:9], heads_ref)
    carry = over_heads(jnp.broadcast_to(jnp.exp(last) * marks[Q - 1 : Q, 7:8], (8, LANES)), heads_ref)
    held[...] = state * carry[0:1, :] + nn(b.T, (x_step * tail).astype(BF16))
    lane = lax.broadcasted_iota(jnp.int32, (Q, LANES), 1)
    for pair in range(MYH // 2):
        cols = slice(pair * LANES, (pair + 1) * LANES)
        mixing = []
        for head in (2 * pair, 2 * pair + 1):
            spread = cum[:, head : head + 1] - cum_t[head : head + 1, :] + shut
            mixing.append((jnp.exp(spread) * scores).astype(BF16))
        steps = x_step[:, cols]
        both = jnp.concatenate(
            [jnp.where(lane < HD, steps, 0.0), jnp.where(lane < HD, 0.0, steps)], axis=0
        ).astype(BF16)
        y_ref[:, cols] = y[:, cols] + nn(jnp.concatenate(mixing, axis=1), both)


def scan_backward(
    group, side_ref, x_ref, x_halo, bc_ref, dt_ref, dy_ref, state_ref, marks_ref, row_ref, x_taps, head_ref, heads_ref,
    *rest,
):
    final = group == GROUPS - 1
    if group > 0:
        dbc_before, *rest = rest
    if final:
        bc_raw_ref, bc_halo, bc_taps, *rest = rest
    dx_ref, dbc_ref, ddt_ref, wide_ref, thin_ref, *rest = rest
    if final:
        bc_sums, *rest = rest
    ext, held, ahead, *rest = rest
    if final:
        bc_ext, bc_ahead = rest
    chunk = pl.program_id(0)

    @pl.when(chunk == 0)
    def _():
        held[...] = jnp.zeros_like(held)
        ahead[...] = jnp.zeros_like(ahead)
        if final:
            bc_ahead[...] = jnp.zeros_like(bc_ahead)

    @pl.when(chunk == 0)
    def _():
        wide_ref[...] = jnp.zeros_like(wide_ref)
        thin_ref[...] = jnp.zeros_like(thin_ref)
        if final:
            bc_sums[...] = jnp.zeros_like(bc_sums)

    marks = marks_ref[...]
    total = conv_total(ext, x_ref, x_halo, x_taps, marks)
    gate = lax.logistic(total)
    x_act = total * gate
    slope = gate * (1.0 + total * (1.0 - gate))
    b, c = bc_ref[:, :NS], bc_ref[:, NS:]
    at_row = lax.broadcasted_iota(jnp.int32, (Q, Q), 0)
    at_col = lax.broadcasted_iota(jnp.int32, (Q, Q), 1)
    lower = (at_row >= at_col).astype(F32)
    shifted, step, rate, log_decay, cum = decays(dt_ref, head_ref, lower)
    cum_t = cum.T
    shut = jnp.where((at_row <= at_col) & (marks[:, 0:1] == row_ref[0]), 0.0, FAR)
    scores = nt(b, c)
    last = cum[Q - 1 : Q, :]
    dy = dy_ref[...].astype(F32)
    step_wide = over_heads(step, heads_ref)
    x_step = x_act * step_wide
    keep = over_heads(jnp.exp(cum) * marks[:, 7:8], heads_ref)
    tail = over_heads(jnp.exp(last - cum) * marks[:, 8:9], heads_ref)
    carry_thin = jnp.broadcast_to(jnp.exp(last) * marks[Q - 1 : Q, 7:8], (8, LANES))
    carry = over_heads(carry_thin, heads_ref)
    state = state_ref[0]
    d_state = held[...]
    d_state_low = d_state.astype(BF16)
    dy_keep = dy * keep
    dy_keep_low = dy_keep.astype(BF16)
    from_state = nn(c, state)
    seen = sum_heads(dy_keep * from_state, heads_ref)
    d_c = nt(dy_keep_low, state)
    to_state = x_step * tail
    d_b = nt(to_state.astype(BF16), d_state_low)
    du_tail = nn(b, d_state_low) * tail
    sent = sum_heads(x_step * du_tail, heads_ref)
    linked = jnp.sum(d_state * state.astype(F32), axis=0, keepdims=True)
    linked = sum_heads(jnp.broadcast_to(linked, (8, GC)), heads_ref)[0:1, :] * carry_thin[0:1, :]
    held[...] = d_state * carry[0:1, :] + nn(c.T, dy_keep_low)
    lane = lax.broadcasted_iota(jnp.int32, (Q, LANES), 1)
    d_scores = jnp.zeros((Q, Q), F32)
    by_later, by_earlier, du_parts = [], [], []
    for pair in range(GH // 2):
        cols = slice(pair * LANES, (pair + 1) * LANES)
        steps, dys = x_step[:, cols], dy[:, cols]
        step_both = jnp.concatenate(
            [jnp.where(lane < HD, steps, 0.0), jnp.where(lane < HD, 0.0, steps)], axis=0
        ).astype(BF16)
        dy_both = jnp.concatenate(
            [jnp.where(lane < HD, dys, 0.0), jnp.where(lane < HD, 0.0, dys)], axis=0
        ).astype(BF16)
        met = nt(step_both, dys.astype(BF16))
        mixing = []
        for place, head in enumerate((group * GH + 2 * pair, group * GH + 2 * pair + 1)):
            decay = jnp.exp(cum_t[head : head + 1, :] - cum[:, head : head + 1] + shut)
            mixing.append((decay * scores).astype(BF16))
            weighed = decay * met[place * Q : (place + 1) * Q, :]
            d_scores = d_scores + weighed
            spent = weighed * scores
            by_later.append(jnp.sum(spent, axis=0, keepdims=True))
            by_earlier.append(jnp.sum(spent, axis=1, keepdims=True))
        du_parts.append(nn(jnp.concatenate(mixing, axis=1), dy_both))
    du = jnp.concatenate(du_parts, axis=1) + du_tail
    d_low = d_scores.astype(BF16)
    d_b = d_b + nn(d_low, c)
    d_c = d_c + nn(d_scores.T.astype(BF16), b)
    d_bc = jnp.concatenate([d_b, d_c], axis=1)
    if group > 0:
        d_bc = d_bc + dbc_before[...]
    if final:
        bc_total = conv_total(bc_ext, bc_raw_ref, bc_halo, bc_taps, marks)
        bc_gate = lax.logistic(bc_total)
        d_bc = d_bc * (bc_gate * (1.0 + bc_total * (1.0 - bc_gate)))
        d_bc = conv_back(d_bc, bc_ext, bc_ahead, bc_taps, marks, bc_sums)
    dbc_ref[...] = d_bc.astype(dbc_ref.dtype)
    low_lanes, high_lanes = group * GH, LANES - (group + 1) * GH
    later = by_later + [jnp.zeros((high_lanes, Q), F32)]
    later = ([jnp.zeros((low_lanes, Q), F32)] if low_lanes else []) + later
    later = jnp.concatenate(later, axis=0).T
    earlier = jnp.zeros((Q, LANES), F32)
    for head in range(GH):
        earlier = jnp.where(lane == low_lanes + head, by_earlier[head], earlier)
    upper = (at_row <= at_col).astype(F32)
    strict = (at_row > at_col).astype(F32)
    d_log = exact(upper, seen + later - earlier) + exact(strict, sent) + linked
    d_step = sum_heads(x_act * du, heads_ref)
    d_raw = (d_step + rate * d_log) * lax.logistic(shifted)
    mine = ((lane >= low_lanes) & (lane < low_lanes + GH)).astype(F32)
    d_raw = d_raw * mine
    ddt_ref[...] = d_raw
    thin_ref[0:1, :] += jnp.sum(d_raw, axis=0, keepdims=True)
    thin_ref[1:2, :] += jnp.sum(d_log * log_decay * mine, axis=0, keepdims=True)
    wide_ref[5:6, :] += jnp.sum(dy * x_act, axis=0, keepdims=True)
    d_total = (du * step_wide + dy * x_taps[5:6, :]) * slope
    dx_ref[...] = conv_back(d_total, ext, ahead, x_taps, marks, wide_ref).astype(BF16)


def block_at(seq, time, side):
    blocks = LEN // Q
    return seq * blocks + (time + side * (blocks // 2)) % blocks


def halo_at(seq, time, side):
    return block_at(seq, jnp.maximum(time - 1, 0), side) * (Q // 16) + Q // 16 - 1


BC_AT = MYC // BC
DT_AT = (MYC + BC) // LANES


def run_forward(side, first, marks, rows, x_taps, bc_taps, head_rows, heads):
    total = first.shape[0]
    blocks = LEN // Q
    here = lambda col: lambda s, t, side: (block_at(s, t, side[0]), col)
    halo = lambda col: lambda s, t, side: (halo_at(s, t, side[0]), col)
    still = lambda s, t, side: (0, 0)
    return pl.pallas_call(
        scan_forward,
        grid_spec=pltpu.PrefetchScalarGridSpec(
            num_scalar_prefetch=1,
            grid=(total // LEN, blocks),
            in_specs=[
                pl.BlockSpec((Q, MYC), here(0)),
                pl.BlockSpec((16, MYC), halo(0)),
                pl.BlockSpec((Q, BC), here(BC_AT)),
                pl.BlockSpec((16, BC), halo(BC_AT)),
                pl.BlockSpec((Q, LANES), here(DT_AT)),
                pl.BlockSpec((Q, 16), lambda s, t, side: (s * blocks + t, 0)),
                pl.BlockSpec((1, 1, Q), lambda s, t, side: (s * blocks + t, 0, 0)),
                pl.BlockSpec((8, MYC), still),
                pl.BlockSpec((8, BC), still),
                pl.BlockSpec((8, LANES), still),
                pl.BlockSpec((2 * LANES, MYC), still),
            ],
            out_specs=[
                pl.BlockSpec((Q, MYC), here(0)),
                pl.BlockSpec((1, NS, MYC), lambda s, t, side: (s * blocks + t, 0, 0)),
                pl.BlockSpec((Q, BC), here(0)),
            ],
            scratch_shapes=[
                pltpu.VMEM((Q + 8, MYC), F32),
                pltpu.VMEM((Q + 8, BC), F32),
                pltpu.VMEM((NS, MYC), F32),
            ],
        ),
        out_shape=[
            jax.ShapeDtypeStruct((total, MYC), F32),
            jax.ShapeDtypeStruct((total // Q, NS, MYC), BF16),
            jax.ShapeDtypeStruct((total, BC), BF16),
        ],
        compiler_params=pltpu.CompilerParams(vmem_limit_bytes=VMEM_LIMIT),
        cost_estimate=pl.CostEstimate(flops=20 * 10**9, bytes_accessed=60 * 10**6, transcendentals=10**7),
        name="scan_forward",
    )(side, first, first, first, first, first, marks, rows, x_taps, bc_taps, head_rows, heads)


def run_backward(group, seq, side, first, bc_act, d_ssm, states, marks, rows, x_taps, bc_taps, head_rows, heads, d_bc):
    blocks = LEN // Q
    final = group == GROUPS - 1
    here = lambda col: lambda t, side: (block_at(seq, blocks - 1 - t, side[0]), col)
    out = lambda t, side: (block_at(0, blocks - 1 - t, side[0]), 0)
    halo = lambda col: lambda t, side: (halo_at(seq, blocks - 1 - t, side[0]), col)
    time = lambda t: seq * blocks + blocks - 1 - t
    still = lambda t, side: (0, 0)
    share = lambda t, side: (0, group)
    in_specs = [
        pl.BlockSpec((Q, GC), here(group)),
        pl.BlockSpec((16, GC), halo(group)),
        pl.BlockSpec((Q, BC), here(0)),
        pl.BlockSpec((Q, LANES), here(DT_AT)),
        pl.BlockSpec((Q, GC), here(group)),
        pl.BlockSpec((1, NS, GC), lambda t, side: (time(t), 0, group)),
        pl.BlockSpec((Q, 16), lambda t, side: (time(t), 0)),
        pl.BlockSpec((1, 1, Q), lambda t, side: (time(t), 0, 0)),
        pl.BlockSpec((8, GC), share),
        pl.BlockSpec((8, LANES), still),
        pl.BlockSpec((2 * LANES, GC), share),
    ]
    inputs = [first, first, bc_act, first, d_ssm, states, marks, rows, x_taps, head_rows, heads]
    out_specs = [
        pl.BlockSpec((Q, GC), out),
        pl.BlockSpec((Q, BC), out),
        pl.BlockSpec((Q, LANES), out),
        pl.BlockSpec((8, GC), still),
        pl.BlockSpec((8, LANES), still),
    ]
    out_shape = [
        jax.ShapeDtypeStruct((LEN, GC), BF16),
        jax.ShapeDtypeStruct((LEN, BC), BF16 if final else F32),
        jax.ShapeDtypeStruct((LEN, LANES), F32),
        jax.ShapeDtypeStruct((8, GC), F32),
        jax.ShapeDtypeStruct((8, LANES), F32),
    ]
    scratch = [pltpu.VMEM((Q + 8, GC), F32), pltpu.VMEM((NS, GC), F32), pltpu.VMEM((8, GC), F32)]
    if group > 0:
        in_specs.append(pl.BlockSpec((Q, BC), out))
        inputs.append(d_bc)
    if final:
        in_specs += [
            pl.BlockSpec((Q, BC), here(BC_AT)),
            pl.BlockSpec((16, BC), halo(BC_AT)),
            pl.BlockSpec((8, BC), still),
        ]
        inputs += [first, first, bc_taps]
        out_specs.append(pl.BlockSpec((8, BC), still))
        out_shape.append(jax.ShapeDtypeStruct((8, BC), F32))
        scratch += [pltpu.VMEM((Q + 8, BC), F32), pltpu.VMEM((8, BC), F32)]
    return pl.pallas_call(
        functools.partial(scan_backward, group),
        grid_spec=pltpu.PrefetchScalarGridSpec(
            num_scalar_prefetch=1, grid=(blocks,), in_specs=in_specs, out_specs=out_specs, scratch_shapes=scratch
        ),
        out_shape=out_shape,
        compiler_params=pltpu.CompilerParams(vmem_limit_bytes=VMEM_LIMIT),
        cost_estimate=pl.CostEstimate(flops=15 * 10**9, bytes_accessed=50 * 10**6, transcendentals=10**7),
        name="scan_backward_%d_%d" % (group, seq),
    )(side, *inputs)


def lead(value, by):
    if by == 0:
        return value
    pad = [(0, 0)] * value.ndim
    if by > 0:
        pad[1] = (0, by)
        return jnp.pad(value, pad)[:, by:]
    pad[1] = (-by, 0)
    return jnp.pad(value, pad)[:, :by]


def fold(block):
    return jnp.concatenate([block[..., : D // 2], block[..., D // 2 :]], axis=-2)


def unfold(block):
    half = block.shape[-2] // 2
    return jnp.concatenate([block[..., :half, :], block[..., half:, :]], axis=-1)


def out_rows(full, core):
    count, rows, cols = full.shape
    full = full.reshape(2, count // 2, rows, cols)
    kept, got = pick(full, core), swap(pick(full, 1 - core), "core")
    first = jnp.where(core == 0, kept, got)
    second = jnp.where(core == 0, got, kept)
    return jnp.stack([unfold(first), unfold(second)], axis=1).reshape(MYC, D)


def out_blocks(grad, count, core):
    rows = DI // (count * PARTS)
    halves = grad.astype(BF16).reshape(count // 2, 2, rows, D)
    kept, got = pick(halves, core, 1), swap(pick(halves, 1 - core, 1), "core")
    first = jnp.where(core == 0, kept, got)
    second = jnp.where(core == 0, got, kept)
    return fold(jnp.concatenate([first, second], axis=0))


def out_whole(out_weight, split, core, side):
    whole = lax.all_gather(out_weight, ("zy", "core", "seq"), axis=0, tiled=True)
    return pick(pick(split_heads(whole, 0, split), core), side)


def out_scattered(grad, split, core, side):
    own = jnp.zeros((2, 2, MYC, D), BF16)
    own = lax.dynamic_update_slice(own, grad.astype(BF16)[None, None], (core, side, 0, 0))
    whole = join_heads(own, 0, split)
    return lax.psum_scatter(whole, ("zy", "core", "seq"), scatter_dimension=0, tiled=True)


def own_slice(whole, size):
    at = (lax.axis_index("zy") * 2 + lax.axis_index("core")) * 2 + lax.axis_index("seq")
    return lax.dynamic_slice_in_dim(whole, at * size, size, 0)


def body(
    tokens,
    segments,
    norm_gain,
    in_weight,
    conv_weight,
    conv_bias,
    dt_bias,
    a_log,
    d_skip,
    gated_gain,
    out_weight,
    cotangent,
):
    count = lax.axis_size("zy")
    core, side = lax.axis_index("core"), lax.axis_index("seq")
    split = head_split(count)
    rows = tokens.shape[1]
    total = PARTS * rows

    blocked = split[0] > 1

    sizes = (norm_gain.shape[0], conv_weight.size, conv_bias.shape[0], gated_gain.shape[0])
    small = jnp.concatenate([norm_gain, conv_weight.reshape(-1), conv_bias, gated_gain])
    me = (core * 2 + side).astype(jnp.int32).reshape(1)
    at_side = side.astype(jnp.int32).reshape(1)
    small = Task(small_steps(small, core, side))
    segs = Task(group_steps(segments[0].reshape(-1, LANES)))

    mix = Task(peer_steps(split_columns(in_weight, split, me)))
    stage([mix, segs, small])
    sent, later = assemble_rows(mix.value, me)
    if blocked:
        held = lax.ppermute(out_weight, GROUP, DIAGONAL)
        later = jnp.concatenate([later, fold(held)], axis=1)
    else:
        w_out = out_whole(out_weight, split, core, side)
    ring = Task(gather_steps(sent, [0]))
    token_all = Task(token_steps(tokens[0], PIECES))
    while not (ring.done and token_all.done and small.done):
        stage([ring, token_all, small])
    w_first = ring.value[0].reshape(D, W1)

    small = small.value.reshape(-1, sum(sizes))
    cuts = np.cumsum(sizes)[:-1]
    gain, taps, bias, gated = (v.reshape(-1).astype(F32) for v in jnp.split(small, cuts, axis=1))
    taps = taps.reshape(CONV, KW)

    def mine(vector, dim=0):
        return pick(pick(split_heads(vector, dim, split), core, dim), side, dim)

    gated_mine = mine(gated)
    x_taps = jnp.concatenate(
        [
            mine(taps[:DI]).T,
            mine(bias[:DI])[None],
            jnp.repeat(mine(d_skip), HD)[None],
            jnp.zeros((2, MYC), F32),
        ],
        axis=0,
    )
    bc_taps = jnp.concatenate(
        [taps[DI:].T, bias[DI:][None], jnp.zeros((3, BC), F32)], axis=0
    )
    head_rows = jnp.concatenate([mine(dt_bias)[None], mine(a_log)[None]], axis=0)
    head_rows = jnp.pad(head_rows, ((0, 6), (0, LANES - MYH)))
    heads = np.kron(np.eye(LANES, MYH, dtype=np.float32), np.ones((1, HD), np.float32))
    heads = jnp.asarray(np.concatenate([heads, heads], axis=0), BF16)

    segs = jnp.stack([v.reshape(-1) for v in segs.value]).reshape(2, 2, rows)
    segs = jnp.where(side == 0, segs, segs[:, ::-1]).reshape(2, LEN).astype(F32)
    before = [lead(segs, k - KW + 1) == segs for k in range(KW - 1)]
    place = jnp.arange(LEN)[None, :]
    before = [(m & (place >= KW - 1 - k)).astype(F32) for k, m in enumerate(before)]
    after = [lead(m, KW - 1 - k) for k, m in enumerate(before)]
    ends = segs.reshape(2, LEN // Q, Q)[:, :, -1:]
    starts = jnp.concatenate([jnp.full((2, 1, 1), -1.0, F32), ends[:, :-1]], axis=1)
    keep = (segs.reshape(2, LEN // Q, Q) == starts).astype(F32).reshape(2, LEN)
    tail = (segs.reshape(2, LEN // Q, Q) == ends).astype(F32).reshape(2, LEN)
    marks = jnp.stack([segs] + before + after + [keep, tail] + [jnp.zeros_like(segs)] * 7, axis=-1)
    marks = marks.reshape(total, 16)
    seg_rows = segs.reshape(total // Q, 1, Q)

    near, far, both = token_all.value
    ring = Task(gather_steps(later, [0, MYC] if blocked else [0]))
    cot_all = Task(token_steps(cotangent[0], 3))
    first, normed, turned = stage(
        [ring, cot_all], project, tokens[0], near, far, both, gain[None], w_first
    )
    scanned = stage(
        [ring, cot_all], run_forward, at_side, first, marks, seg_rows, x_taps, bc_taps, head_rows, heads
    )
    while not (ring.done and cot_all.done):
        stage([ring, cot_all])
    y, states, bc_act = scanned
    near, far, both = cot_all.value
    cot_all = jnp.concatenate([cotangent[0]] + far + [near] + both, axis=0)
    w_gate = ring.value[0].reshape(D, MYC)
    if blocked:
        w_out = out_rows(ring.value[1], core)

    gate = nn(normed, w_gate).astype(BF16).astype(F32)
    sig = lax.logistic(gate)
    silu = gate * sig
    joined = y * silu
    d_two = nt(cot_all, w_out)
    sums = jnp.stack(
        [jnp.sum(joined * joined, axis=-1), jnp.sum(joined * gated_mine * d_two, axis=-1)]
    )
    sums = sums.reshape(2, 2, 2, rows)
    sums = sums + swap(sums, "core")[:, ::-1]
    sums = (sums + swap(sums, "seq")[:, :, ::-1]).reshape(2, total)
    inv_two = lax.rsqrt(sums[0] / DI + EPS)[:, None]
    mean_two = (sums[1] / DI)[:, None]
    two = (joined * inv_two * gated_mine).astype(BF16)
    d_joined = inv_two * (gated_mine * d_two) - joined * (inv_two * inv_two * inv_two * mean_two)
    d_ssm = (d_joined * silu).astype(BF16)
    d_gate = (d_joined * y * (sig * (1.0 + gate * (1.0 - sig)))).astype(BF16)
    d_gated = jnp.sum(joined * inv_two * d_two, axis=0)

    def tn(a, b):
        return lax.dot_general(a, b, (((0,), (0,)), ((), ())), preferred_element_type=F32)

    two, d_ssm, d_gate = lax.optimization_barrier((two, d_ssm, d_gate))
    branch = nn(two, w_out).astype(BF16).reshape(PARTS, rows, D)
    d_out = tn(two, cot_all)
    d_w_gate = nn(turned, d_gate).astype(BF16).reshape(count, D // count, MYC)
    if blocked:
        d_out = out_blocks(d_out, count, core)
        d_w_gate = jnp.concatenate([d_w_gate, d_out], axis=2)
    ring = Task(scatter_steps(d_w_gate))
    branch = Task(sum_steps(branch, 2))

    def back(group, seq, d_bc):
        return (
            functools.partial(run_backward, group, seq),
            at_side, first, bc_act, d_ssm, states, marks, seg_rows, x_taps, bc_taps, head_rows, heads, d_bc,
        )

    def weights(pieces):
        return nn(turned, jnp.concatenate(pieces, axis=0))

    parts = {}
    for seq in range(2):
        parts[0, seq] = stage([ring, branch], *back(0, seq, None))
    early = weights([parts[0, 0][0], parts[0, 1][0]]).reshape(count, D // count, GC)
    early = Task(scatter_steps(early))
    for seq in range(2):
        parts[1, seq] = stage([ring, branch, early], *back(1, seq, parts[0, seq][1]))
    d_dt = [parts[0, seq][2] + parts[1, seq][2] for seq in range(2)]
    d_rest = [jnp.concatenate([parts[1, seq][0], parts[1, seq][1], d_dt[seq].astype(BF16)], axis=1) for seq in range(2)]
    wide = jnp.concatenate([parts[g, 0][3] + parts[g, 1][3] for g in range(GROUPS)], axis=1)
    thin = sum(parts[g, seq][4] for g in range(GROUPS) for seq in range(2))
    bc_sums = parts[1, 0][5] + parts[1, 1][5]
    d_w_rest = stage([ring, branch, early], weights, d_rest).reshape(count, D // count, W1 - GC)
    rest = Task(scatter_steps(d_w_rest))

    d_first = [[parts[0, seq][0], d_rest[seq]] for seq in range(2)]

    def partial_normed(pieces, b, at, w1, w2):
        def rows_of(value, start=0):
            return value[start + at * rows : start + (at + 1) * rows]

        a0 = jnp.concatenate([rows_of(p[0]) for p in pieces], axis=0)
        a1 = jnp.concatenate([rows_of(p[1]) for p in pieces], axis=0)
        b = jnp.concatenate([rows_of(b), rows_of(b, 2 * rows)], axis=0)
        value = nt(a0, w1[:, :GC]) + nt(a1, w1[:, GC:]) + nt(b, w2)
        return value.astype(BF16).reshape(2, rows, D)

    def partial_of(at):
        return (lambda *a: partial_normed(a[0], a[1], at, a[2], a[3])), d_first, d_gate, w_first, w_gate

    far = stage([rest, early, ring, branch], *partial_of(1))
    far = Task(far_steps(far, 2))
    near = stage([rest, early, ring, far], *partial_of(0))
    near = Task(far_steps(near, 0))
    small_grads = Task(small_sum_steps(
        (
            wide[:KW].reshape(-1),
            wide[KW],
            d_gated,
            bc_sums[: KW + 1].reshape(-1),
            thin[0, :MYH],
            thin[1, :MYH],
            jnp.sum(wide[KW + 1].reshape(MYH, HD), axis=1),
        ),
        core, side,
    ))
    stage([rest, early, ring, far, near, small_grads])
    finish([rest, early, ring, far, small_grads])
    d_normed = near.value + far.value.astype(F32)

    d_w = Task(peer_steps(hand_back([early.value, rest.value, ring.value[:, :MYC]], me)))
    if blocked:
        d_out = unfold(ring.value[:, MYC:].astype(BF16))
        d_out = lax.ppermute(d_out, GROUP, DIAGONAL).astype(F32)
    else:
        d_out = out_scattered(d_out, split, core, side).astype(F32)
    finish([d_w])
    in_sh = join_columns(d_w.value, split, me)
    block_out = (tokens[0].astype(F32) + branch.value).astype(BF16)[None]

    x = tokens[0].astype(F32)
    inv = lax.rsqrt(jnp.mean(x * x, axis=-1, keepdims=True) + EPS)
    scaled = gain * d_normed
    input_grad = (
        cotangent[0].astype(F32)
        + inv * scaled
        - x * (inv * inv * inv * jnp.mean(x * scaled, axis=-1, keepdims=True))
    )[None]
    d_gain = jnp.sum(x * inv * d_normed, axis=0)

    taps_x, bias_x, gain_two, taps_bc, bias_dt, alog, skip = small_grads.value
    taps_x = jnp.swapaxes(taps_x.reshape(2, 2, KW, MYC), 2, 3)
    taps_bc = jnp.sum(taps_bc, axis=(0, 1)).reshape(KW + 1, BC)
    conv_w = jnp.concatenate([join_heads(taps_x, 0, split), taps_bc[:KW].T], axis=0)
    conv_b = jnp.concatenate([join_heads(bias_x, 0, split), taps_bc[KW]])
    d_gain = jnp.pad(d_gain, (0, -D % 1024)).reshape(-1, LANES)
    d_gain = zy_sum(d_gain)
    d_gain = d_gain + swap(d_gain, "core")
    d_gain = (d_gain + swap(d_gain, "seq")).reshape(-1)[:D]
    return (
        block_out,
        input_grad,
        own_slice(d_gain, norm_gain.shape[0]),
        in_sh,
        own_slice(conv_w, conv_bias.shape[0]),
        own_slice(conv_b, conv_bias.shape[0]),
        join_heads(bias_dt, 0, split),
        join_heads(alog, 0, split),
        join_heads(skip, 0, split),
        own_slice(join_heads(gain_two, 0, split), gated_gain.shape[0]),
        d_out,
    )


def solution(mesh):
    fsdp, seq = mesh.shape["fsdp"], mesh.shape["seq"]
    grid = Mesh(mesh.devices.reshape(fsdp // 2, 2, seq), ("zy", "core", "seq"))
    every = ("zy", "core", "seq")
    rows = P(("zy", "core"), "seq", None)
    in_specs = (
        rows,
        P(("zy", "core"), "seq"),
        P(every),
        P(every, None),
        P(every, None),
        P(every),
        P(),
        P(),
        P(),
        P(every),
        P(every, None),
        rows,
    )
    out_specs = (
        rows,
        rows,
        P(every),
        P(every, None),
        P(every, None),
        P(every),
        P(),
        P(),
        P(),
        P(every),
        P(every, None),
    )
    return jax.shard_map(body, mesh=grid, in_specs=in_specs, out_specs=out_specs, check_vma=False)
```

time: 654 us -> 514 us (0.79)
  waiting for transfers between devices: 188 us -> 62.9 us
  Pallas kernels: 69.3 us -> 130 us
  matrix products: 89.9 us -> 64 us
  between operations: 25.8 us -> 3.51 us
  starting transfers between devices: 102 us -> 88.4 us
  local copies, waits for them, and re-layouts: 102 us -> 91.5 us
    ppermute x29 -> x6, waiting for transfers between devices: 77.4 us -> 10.4 us  [swap(): return lax.ppermute(value, axis, SWAP)]
    pallas_call x2 -> x10, Pallas kernels: 69.3 us -> 130 us  [the longest x4 78.6 us: run_backward(): pl.pallas_call(functools.partial(scan_backward, group), grid_spec=pltpu.P...]
    ppermute x50 -> x85, waiting for transfers between devices: 103 us -> 50.8 us  [the longest x83 50.8 us: stage(): lax.ppermute(v, m[1], m[2])]
    ppermute x29 -> x6, starting transfers between devices: 27.3 us -> 3.76 us  [swap(): return lax.ppermute(value, axis, SWAP)]
    dot_general x3 -> x1, matrix products: 25.6 us -> 5.47 us  [tn(): lax.dot_general(a, b, (((0,), (0,)), ((), ())), preferred_element_type=F32)]
    ppermute x50 -> x85, starting transfers between devices: 63.2 us -> 82.8 us  [the longest x83 78.4 us: stage(): lax.ppermute(v, m[1], m[2])]
    unnamed x168 -> x191, local copies, waits for them, and re-layouts: 9.04 us -> 26.6 us
    convert_element_type x9 -> x3, local copies, waits for them, and re-layouts: 16.7 us -> 0.65 us  [body(): segs = jnp.where(side == 0, segs, segs[:, ::-1]).reshape(2, LEN).astype(F32)]
  transfers between devices with their start and end apart: 85 -> 94, of which waited for: 49 -> 17; matrix products, arithmetic and copies ran while one was open for 27% -> 25% of each run, Pallas kernels for 0% -> 25%
where the time goes in v2:
time: 514 us; the launch traced here: 504 us
  Pallas kernels  130 us (25%)
  local copies, waits for them, and re-layouts  91.5 us (18%)
  starting transfers between devices  88.4 us (17%)
  other arithmetic  64 us (12%)
  matrix products  64 us (12%)
  waiting for transfers between devices  62.9 us (12%)
    pallas_call x4, Pallas kernels, run_backward(): pl.pallas_call(functools.partial(scan_backward, group), grid_spec=pltpu.P...  78.6 us
    ppermute x83, starting transfers between devices, stage(): lax.ppermute(v, m[1], m[2])  78.4 us
    ppermute x83, waiting for transfers between devices, stage(): lax.ppermute(v, m[1], m[2])  50.8 us
    dot_general x5, matrix products, nn(): lax.dot_general(a, b, (((1,), (0,)), ((), ())), preferred_element_type=F32)  30.3 us
    dot_general x7, matrix products, nt(): lax.dot_general(a, b, (((1,), (1,)), ((), ())), preferred_element_type=F32)  28.3 us
    unnamed x191, local copies, waits for them, and re-layouts  26.6 us
    pallas_call x1, Pallas kernels, run_forward(): pl.pallas_call(scan_forward, grid_spec=pltpu.PrefetchScalarGridSpec(num_s...  22.3 us
    pallas_call x1, Pallas kernels, project(): pl.pallas_call(project_kernel, grid=(total // PROJECT,), in_specs=[pl.Blo...  19.6 us
  transfers between devices with their start and end apart: 94, of which 17 were waited for; matrix products, arithmetic and copies ran while one was open for 25% of the time, Pallas kernels for 25%

profile of v2, /device:TPU:0, one launch (start us, length us, event | category | flops | bytes accessed | tf_op | source)
XLA Modules:
  0.0 504.2 jit_solution(3425080619140773748)
XLA Ops:
  6.7 2.9 collective-permute-start
  26.3 3.7 collective-permute-start.9
  58.3 4.8 collective-permute-done.19
  71.3 6.8 %collective-permute-done.24 = bf16[4,4,664]{2,1,0:T(4,128)(2,1)S(1)} collective-permute-done((bf16[4,4,664]{2,1,0:T(4,128)(2,1)S(1)}, bf16[4,4,664]{2,1,0:T(4,128)(2,1)S(1)}, u32[]{:S(2)}, u32[]{:S(2)}) %collective-permute-start.24) | collective-permute-done | bytes 21280 | tf_op jit(solution)/shard_map/ppermute | solution.py:101
  104.9 19.6 %project.1 = (bf16[2048,1152]{1,0:T(8,128)(2,1)}, bf16[2048,1536]{1,0:T(8,128)(2,1)}, bf16[1536,2048]{1,0:T(8,128)(2,1)}) custom-call(bf16[512,1536]{1,0:T(8,128)(2,1)} %bitcast.394, bf16[512,1536]{1,0:T(8,128)(2,1)} %collective-permute-done.12.refs_1_, bf16[128,1536]{1,0:T(8,128)(2,1)} %collective-permute-done.13.refs_2_, bf16[128,1536]{1,0:T(8,128)(2,1)} %copy-done.73, ...), custom_call_target="tpu_custom_call" | custom-call | flops 12000000000 | bytes 30000000 | tf_op jit(solution)/shard_map/project/pallas_call | solution.py:504
  128.6 22.3 %scan_forward.1 = (f32[2048,768]{1,0:T(8,128)}, bf16[16,128,768]{2,1,0:T(8,128)(2,1)}, bf16[2048,256]{1,0:T(8,128)(2,1)}) custom-call(s32[1]{0:T(128)} %bitcast.26.side_ref, bf16[2048,1152]{1,0:T(8,128)(2,1)} %get-tuple-element.515.x_ref.x_halo.bc_ref.bc_halo.dt_ref.rest_1_.rest_2_, ...), custom_call_target="tpu_custom_call" | custom-call | flops 20000000000 | bytes 60000000 | tf_op jit(solution)/shard_map/scan_forward/pallas_call | solution.py:762
  163.7 9.1 %collective-permute-done.41 = bf16[176,1536]{1,0:T(8,128)(2,1)S(1)} collective-permute-done((bf16[176,1536]{1,0:T(8,128)(2,1)S(1)}, bf16[176,1536]{1,0:T(8,128)(2,1)S(1)}, u32[]{:S(2)}, u32[]{:S(2)}) %collective-permute-start.41) | collective-permute-done | bytes 540704 | tf_op jit(solution)/shard_map/ppermute | solution.py:101
  183.9 5.2 %convolution_convert_fusion.3 = bf16[2048,768]{1,0:T(8,128)(2,1)S(1)} fusion(bf16[2048,1536]{1,0:T(8,128)(2,1)S(1)} %bitcast.476, bf16[1536,768]{1,0:T(8,128)(2,1)S(1)} %bitcast.415), kind=kOutput, calls=%fused_computation.35 | convolution fusion | flops 4833411072 | bytes 11796480 | tf_op jit(solution)/shard_map/dot_general | solution.py:445
  195.8 8.2 %multiply_reduce_fusion.1 = (f32[2048]{0:T(1024)S(1)}, f32[2048]{0:T(1024)S(1)}, f32[2048,768]{1,0:T(8,128)}) fusion(f32[768]{0:T(1024)S(1)} %fusion.109, f32[2048,768]{1,0:T(8,128)S(1)} %bitcast.406, bf16[2048,768]{1,0:T(8,128)(2,1)S(1)} %convolution_convert_fusion.3, bf16[2048,1536]{1,0:T(8,128)(2,1)S(1)} %copy-done.43, bf16[768,1536]{1,0:T(8,128)(2,1)S(1)} %bitcast.418), kind=kOutput, calls=%fused_computation.24 | convolution fusion | flops 4849135616 | bytes 24398848 | tf_op jit(solution)/shard_map/dot_general | solution.py:441
  209.3 11.2 %fusion.11 = (bf16[2048,768]{1,0:T(8,128)(2,1)S(1)}, bf16[2048,768]{1,0:T(8,128)(2,1)}, f32[768]{0:T(1024)S(1)}, bf16[2048,768]{1,0:T(8,128)(2,1)S(1)}) fusion(bf16[2048,768]{1,0:T(8,128)(2,1)} %copy-done.12, f32[2048,768]{1,0:T(8,128)} %get-tuple-element.409, f32[2048]{0:T(1024)S(1)} %fusion.102, f32[2048,768]{1,0:T(8,128)} %get-tuple-element.729, ...), kind=kLoop, calls=%fused_computation.17 | loop fusion | flops 37747968 | bytes 25188352 | tf_op jit(solution)/shard_map/convert_element_type | solution.py:1037
  220.5 5.2 %convolution_convert_fusion = bf16[2048,1536]{1,0:T(8,128)(2,1)S(1)} fusion(bf16[2048,768]{1,0:T(8,128)(2,1)S(1)} %get-tuple-element.430, bf16[768,1536]{1,0:T(8,128)(2,1)S(1)} %bitcast.419), kind=kOutput, calls=%fused_computation.8 | convolution fusion | flops 4834983936 | bytes 11796480 | tf_op jit(solution)/shard_map/dot_general | solution.py:445
  225.8 5.5 %convolution_convert_fusion.1 = bf16[768,1536]{1,0:T(8,128)(2,1)S(1)} fusion(bf16[2048,768]{1,0:T(8,128)(2,1)S(1)} %get-tuple-element.430, bf16[2048,1536]{1,0:T(8,128)(2,1)S(1)} %bitcast.434), kind=kOutput, calls=%fused_computation.33 | convolution fusion | flops 4833017856 | bytes 11796480 | tf_op jit(solution)/shard_map/dot_general | solution.py:1041
  233.3 5.6 %convolution_convert_fusion.2 = bf16[1536,768]{1,0:T(8,128)(2,1)S(1)} fusion(bf16[1536,2048]{1,0:T(8,128)(2,1)S(1)} %bitcast.474, bf16[2048,768]{1,0:T(8,128)(2,1)S(1)} %get-tuple-element.571), kind=kOutput, calls=%fused_computation.34 | convolution fusion | flops 4833017856 | bytes 11796480 | tf_op jit(solution)/shard_map/dot_general | solution.py:445
  239.2 2.8 fusion.14
  249.1 18.0 %scan_backward_0_0.1 = (bf16[1024,384]{1,0:T(8,128)(2,1)}, f32[1024,256]{1,0:T(8,128)}, f32[1024,128]{1,0:T(8,128)}, f32[8,384]{1,0:T(8,128)}, f32[8,128]{1,0:T(8,128)}) custom-call(s32[1]{0:T(128)} %bitcast.26.side_ref, bf16[2048,1152]{1,0:T(8,128)(2,1)} %get-tuple-element.515.x_ref.x_halo.bc_ref.bc_halo.dt_ref.rest_1_.rest_2_, ...), custom_call_target="tpu_custom_call" | custom-call | flops 15000000512 | bytes 50000000 | tf_op jit(solution)/shard_map/scan_backward_0_0/pallas_call | solution.py:853
  278.7 18.1 %scan_backward_0_1.1 = (bf16[1024,384]{1,0:T(8,128)(2,1)}, f32[1024,256]{1,0:T(8,128)}, f32[1024,128]{1,0:T(8,128)}, f32[8,384]{1,0:T(8,128)}, f32[8,128]{1,0:T(8,128)}) custom-call(s32[1]{0:T(128)} %bitcast.26.side_ref, bf16[2048,1152]{1,0:T(8,128)(2,1)} %get-tuple-element.515.x_ref.x_halo.bc_ref.bc_halo.dt_ref.rest_1_.rest_2_, ...), custom_call_target="tpu_custom_call" | custom-call | flops 15000000512 | bytes 50000000 | tf_op jit(solution)/shard_map/scan_backward_0_1/pallas_call | solution.py:853
  296.8 5.7 %fusion.36 = f32[1536,384]{1,0:T(8,128)S(1)} fusion(bf16[1536,2048]{1,0:T(8,128)(2,1)} %get-tuple-element.431, bf16[1024,384]{1,0:T(8,128)(2,1)} %get-tuple-element.567, bf16[1024,384]{1,0:T(8,128)(2,1)S(1)} %copy-done.25), kind=kOutput, calls=%fused_computation.65 | convolution fusion | flops 2419064832 | bytes 10223616 | tf_op jit(solution)/shard_map/dot_general | solution.py:445
  304.6 2.9 fusion.58
  313.3 21.2 %scan_backward_1_0.1 = (bf16[1024,384]{1,0:T(8,128)(2,1)}, bf16[1024,256]{1,0:T(8,128)(2,1)}, f32[1024,128]{1,0:T(8,128)}, f32[8,384]{1,0:T(8,128)}, f32[8,128]{1,0:T(8,128)}, /*index=5*/f32[8,256]{1,0:T(8,128)}) custom-call(s32[1]{0:T(128)} %bitcast.26.side_ref, bf16[2048,1152]{1,0:T(8,128)(2,1)} %get-tuple-element.515.x_ref.x_halo.bc_ref.bc_halo.dt_ref.rest_1_.rest_2_, ...), custom_call_target="tpu_custom_call" | custom-call | flops 15000000512 | bytes 50000000 | tf_op jit(solution)/shard_map/scan_backward_1_0/pallas_call | solution.py:853
  334.7 2.9 fusion.56
  344.8 21.2 %scan_backward_1_1.1 = (bf16[1024,384]{1,0:T(8,128)(2,1)}, bf16[1024,256]{1,0:T(8,128)(2,1)}, f32[1024,128]{1,0:T(8,128)}, f32[8,384]{1,0:T(8,128)}, f32[8,128]{1,0:T(8,128)}, /*index=5*/f32[8,256]{1,0:T(8,128)}) custom-call(s32[1]{0:T(128)} %bitcast.26.side_ref, bf16[2048,1152]{1,0:T(8,128)(2,1)} %get-tuple-element.515.x_ref.x_halo.bc_ref.bc_halo.dt_ref.rest_1_.rest_2_, ...), custom_call_target="tpu_custom_call" | custom-call | flops 15000000512 | bytes 50000000 | tf_op jit(solution)/shard_map/scan_backward_1_1/pallas_call | solution.py:853
  371.5 8.6 %fusion.21 = f32[1536,768]{1,0:T(8,128)} fusion(bf16[1536,2048]{1,0:T(8,128)(2,1)} %get-tuple-element.431, bf16[1024,768]{1,0:T(8,128)(2,1)S(1)} %pad_maximum_fusion.2, bf16[1024,768]{1,0:T(8,128)(2,1)S(1)} %pad_maximum_fusion.1), kind=kOutput, calls=%fused_computation.42 | convolution fusion | flops 4838129664 | bytes 14155776 | tf_op jit(solution)/shard_map/dot_general | solution.py:445
  391.7 4.3 fusion.34
  396.0 3.1 add_convert_fusion.1
  407.4 4.3 fusion.32
  411.7 3.1 add_convert_fusion
  427.9 6.0 %collective-permute-done.77 = f32[48,128]{1,0:T(8,128)S(1)} collective-permute-done((f32[48,128]{1,0:T(8,128)S(1)}, f32[48,128]{1,0:T(8,128)S(1)}, u32[]{:S(2)}, u32[]{:S(2)}) %collective-permute-start.77) | collective-permute-done | bytes 24608 | tf_op jit(solution)/shard_map/ppermute | solution.py:101
  434.7 6.7 %collective-permute-done.75 = bf16[256,1536]{1,0:T(8,128)(2,1)S(1)} collective-permute-done((bf16[256,1536]{1,0:T(8,128)(2,1)}, bf16[256,1536]{1,0:T(8,128)(2,1)S(1)}, u32[]{:S(2)}, u32[]{:S(2)}) %collective-permute-start.75) | collective-permute-done | bytes 786464 | tf_op jit(solution)/shard_map/ppermute | solution.py:101
  447.2 4.5 fusion.30
  457.2 5.5 %collective-permute-done.80 = bf16[256,1536]{1,0:T(8,128)(2,1)S(1)} collective-permute-done((bf16[256,1536]{1,0:T(8,128)(2,1)S(1)}, bf16[256,1536]{1,0:T(8,128)(2,1)S(1)}, u32[]{:S(2)}, u32[]{:S(2)}) %collective-permute-start.80) | collective-permute-done | bytes 786464 | tf_op jit(solution)/shard_map/ppermute | solution.py:101
  465.0 3.9 fusion.18
  483.4 7.3 %collective-permute-done.86 = f32[16,128]{1,0:T(8,128)S(1)} collective-permute-done((f32[16,128]{1,0:T(8,128)S(1)}, f32[16,128]{1,0:T(8,128)S(1)}, u32[]{:S(2)}, u32[]{:S(2)}) %collective-permute-start.86) | collective-permute-done | bytes 8224 | tf_op jit(solution)/shard_map/ppermute | solution.py:43
  (632 shorter events, 240.5 us)
Async XLA Ops:
  6.7 23.4 %collective-permute-start = (bf16[48,1920]{1,0:T(8,128)(2,1)}, bf16[48,1920]{1,0:T(8,128)(2,1)S(1)}, u32[]{:S(2)}, u32[]{:S(2)}) collective-permute-start(bf16[48,1920]{1,0:T(8,128)(2,1)} %get-tuple-element.313), channel_id=1, source_target_pairs={{0,1},{1,0},{2,3},{3,2},{4,5},{5,4},{6,7},{7,6},{8,9},{9,8},{10,11... | collective-permute-start | bytes 552968 | tf_op jit(solution)/shard_map/ppermute | solution.py:101
  9.7 20.4 %collective-permute-start.1 = (bf16[48,1920]{1,0:T(8,128)(2,1)}, bf16[48,1920]{1,0:T(8,128)(2,1)S(1)}, u32[]{:S(2)}, u32[]{:S(2)}) collective-permute-start(bf16[48,1920]{1,0:T(8,128)(2,1)} %get-tuple-element.314), channel_id=1, source_target_pairs={{0,2},{1,3},{2,0},{3,1},{4,6},{5,7},{6,4},{7,5},{8,10},{9,11},{10,... | collective-permute-start | bytes 552968 | tf_op jit(solution)/shard_map/ppermute | solution.py:101
  9.7 20.4 %collective-permute-start.2 = (bf16[48,1920]{1,0:T(8,128)(2,1)}, bf16[48,1920]{1,0:T(8,128)(2,1)}, u32[]{:S(2)}, u32[]{:S(2)}) collective-permute-start(bf16[48,1920]{1,0:T(8,128)(2,1)} %get-tuple-element.315), channel_id=1, source_target_pairs={{0,3},{1,2},{2,1},{3,0},{4,7},{5,6},{6,5},{7,4},{8,11},{9,10},{10,... | collective-permute-start | bytes 552968 | tf_op jit(solution)/shard_map/ppermute | solution.py:101
  99.5 25.0 %collective-permute-start.32 = (bf16[512,1536]{1,0:T(8,128)(2,1)S(1)}, bf16[512,1536]{1,0:T(8,128)(2,1)S(1)}, u32[]{:S(2)}, u32[]{:S(2)}) collective-permute-start(bf16[512,1536]{1,0:T(8,128)(2,1)S(1)} %bitcast.399), channel_id=1, source_target_pairs={{0,2},{2,0},{1,3},{3,1},{4,6},{6,4},{5,7},{7,5},{8,10},{10,8},{9,1... | collective-permute-start | bytes 4718600 | tf_op jit(solution)/shard_map/ppermute | solution.py:101
  101.4 23.2 %collective-permute-start.30 = (bf16[192,1536]{1,0:T(8,128)(2,1)}, bf16[192,1536]{1,0:T(8,128)(2,1)}, u32[]{:S(2)}, u32[]{:S(2)}) collective-permute-start(bf16[192,1536]{1,0:T(8,128)(2,1)} %maximum_maximum_fusion), channel_id=1, source_target_pairs={{0,8},{8,16},{16,24},{24,28},{28,20},{20,12},{12,4},{4,0},{1,9},{9... | collective-permute-start | bytes 1769480 | tf_op jit(solution)/shard_map/ppermute | solution.py:101
  102.7 21.8 %collective-permute-start.31 = (bf16[192,1536]{1,0:T(8,128)(2,1)}, bf16[192,1536]{1,0:T(8,128)(2,1)}, u32[]{:S(2)}, u32[]{:S(2)}) collective-permute-start(bf16[192,1536]{1,0:T(8,128)(2,1)} %maximum_maximum_fusion), channel_id=1, source_target_pairs={{8,0},{16,8},{24,16},{28,24},{20,28},{12,20},{4,12},{0,4},{9,1},{1... | collective-permute-start | bytes 1769480 | tf_op jit(solution)/shard_map/ppermute | solution.py:101
  103.4 21.1 %collective-permute-start.33 = (bf16[160,1536]{1,0:T(8,128)(2,1)}, bf16[160,1536]{1,0:T(8,128)(2,1)}, u32[]{:S(2)}, u32[]{:S(2)}) collective-permute-start(bf16[160,1536]{1,0:T(8,128)(2,1)} %slice_bitcast_fusion.5), channel_id=1, source_target_pairs={{0,1},{1,0},{2,3},{3,2},{4,5},{5,4},{6,7},{7,6},{8,9},{9,8},{10,11... | collective-permute-start | bytes 1474568 | tf_op jit(solution)/shard_map/ppermute | solution.py:101
  124.6 30.5 %collective-permute-start.34 = (bf16[192,1536]{1,0:T(8,128)(2,1)}, bf16[192,1536]{1,0:T(8,128)(2,1)}, u32[]{:S(2)}, u32[]{:S(2)}) collective-permute-start(bf16[192,1536]{1,0:T(8,128)(2,1)} %collective-permute-done.30), channel_id=1, source_target_pairs={{0,8},{8,16},{16,24},{24,28},{28,20},{20,12},{12,4},{4,0},{1,9},{9... | collective-permute-start | bytes 1769480 | tf_op jit(solution)/shard_map/ppermute | solution.py:101
  125.9 29.1 %collective-permute-start.35 = (bf16[192,1536]{1,0:T(8,128)(2,1)}, bf16[192,1536]{1,0:T(8,128)(2,1)S(1)}, u32[]{:S(2)}, u32[]{:S(2)}) collective-permute-start(bf16[192,1536]{1,0:T(8,128)(2,1)} %collective-permute-done.31), channel_id=1, source_target_pairs={{8,0},{16,8},{24,16},{28,24},{20,28},{12,20},{4,12},{0,4},{9,1},{1... | collective-permute-start | bytes 1769480 | tf_op jit(solution)/shard_map/ppermute | solution.py:101
  126.8 28.2 %collective-permute-start.36 = (bf16[160,1536]{1,0:T(8,128)(2,1)}, bf16[160,1536]{1,0:T(8,128)(2,1)}, u32[]{:S(2)}, u32[]{:S(2)}) collective-permute-start(bf16[160,1536]{1,0:T(8,128)(2,1)} %collective-permute-done.33), channel_id=1, source_target_pairs={{0,2},{2,0},{1,3},{3,1},{4,6},{6,4},{5,7},{7,5},{8,10},{10,8},{9,1... | collective-permute-start | bytes 1474568 | tf_op jit(solution)/shard_map/ppermute | solution.py:101
  126.8 28.2 %collective-permute-start.37 = (bf16[176,1536]{1,0:T(8,128)(2,1)}, bf16[176,1536]{1,0:T(8,128)(2,1)S(1)}, u32[]{:S(2)}, u32[]{:S(2)}) collective-permute-start(bf16[176,1536]{1,0:T(8,128)(2,1)} %get-tuple-element.397), channel_id=1, source_target_pairs={{0,1},{1,0},{2,3},{3,2},{4,5},{5,4},{6,7},{7,6},{8,9},{9,8},{10,11... | collective-permute-start | bytes 1622024 | tf_op jit(solution)/shard_map/ppermute | solution.py:101
  245.2 21.9 %collective-permute-start.51 = (bf16[2,512,1536]{2,1,0:T(8,128)(2,1)}, bf16[2,512,1536]{2,1,0:T(8,128)(2,1)}, u32[]{:S(2)}, u32[]{:S(2)}) collective-permute-start(bf16[2,512,1536]{2,1,0:T(8,128)(2,1)} %bitcast.80), channel_id=1, source_target_pairs={{0,2},{2,0},{1,3},{3,1},{4,6},{6,4},{5,7},{7,5},{8,10},{10,8},{9,1... | collective-permute-start | bytes 9437192 | tf_op jit(solution)/shard_map/ppermute | solution.py:101
  245.7 21.4 %collective-permute-start.49 = (bf16[96,1536]{1,0:T(8,128)(2,1)}, bf16[96,1536]{1,0:T(8,128)(2,1)}, u32[]{:S(2)}, u32[]{:S(2)}) collective-permute-start(bf16[96,1536]{1,0:T(8,128)(2,1)} %get-tuple-element.436), channel_id=1, source_target_pairs={{0,8},{8,16},{16,24},{24,28},{28,20},{20,12},{12,4},{4,0},{1,9},{9... | collective-permute-start | bytes 884744 | tf_op jit(solution)/shard_map/ppermute | solution.py:101
  246.1 21.0 %collective-permute-start.50 = (bf16[96,1536]{1,0:T(8,128)(2,1)}, bf16[96,1536]{1,0:T(8,128)(2,1)}, u32[]{:S(2)}, u32[]{:S(2)}) collective-permute-start(bf16[96,1536]{1,0:T(8,128)(2,1)} %get-tuple-element.437), channel_id=1, source_target_pairs={{8,0},{16,8},{24,16},{28,24},{20,28},{12,20},{4,12},{0,4},{9,1},{1... | collective-permute-start | bytes 884744 | tf_op jit(solution)/shard_map/ppermute | solution.py:101
  273.8 23.0 %collective-permute-start.52 = (bf16[192,1536]{1,0:T(8,128)(2,1)}, bf16[192,1536]{1,0:T(8,128)(2,1)}, u32[]{:S(2)}, u32[]{:S(2)}) collective-permute-start(bf16[192,1536]{1,0:T(8,128)(2,1)} %pad_maximum_fusion.3), channel_id=1, source_target_pairs={{0,8},{8,16},{16,24},{24,28},{28,20},{20,12},{12,4},{4,0},{1,9},{9... | collective-permute-start | bytes 1769480 | tf_op jit(solution)/shard_map/ppermute | solution.py:101
  274.2 22.6 %collective-permute-start.53 = (bf16[192,1536]{1,0:T(8,128)(2,1)}, bf16[192,1536]{1,0:T(8,128)(2,1)}, u32[]{:S(2)}, u32[]{:S(2)}) collective-permute-start(bf16[192,1536]{1,0:T(8,128)(2,1)} %pad_maximum_fusion.4), channel_id=1, source_target_pairs={{8,0},{16,8},{24,16},{28,24},{20,28},{12,20},{4,12},{0,4},{9,1},{1... | collective-permute-start | bytes 1769480 | tf_op jit(solution)/shard_map/ppermute | solution.py:101
  275.8 21.0 %collective-permute-start.54 = (bf16[256,1536]{1,0:T(8,128)(2,1)}, bf16[256,1536]{1,0:T(8,128)(2,1)}, u32[]{:S(2)}, u32[]{:S(2)}) collective-permute-start(bf16[256,1536]{1,0:T(8,128)(2,1)} %get-tuple-element.459), channel_id=1, source_target_pairs={{0,1},{1,0},{2,3},{3,2},{4,5},{5,4},{6,7},{7,6},{8,9},{9,8},{10,11... | collective-permute-start | bytes 2359304 | tf_op jit(solution)/shard_map/ppermute | solution.py:101
  307.5 27.2 %collective-permute-start.55 = (bf16[192,1536]{1,0:T(8,128)(2,1)}, bf16[192,1536]{1,0:T(8,128)(2,1)}, u32[]{:S(2)}, u32[]{:S(2)}) collective-permute-start(bf16[192,1536]{1,0:T(8,128)(2,1)} %get-tuple-element.481), channel_id=1, source_target_pairs={{0,8},{8,16},{16,24},{24,28},{28,20},{20,12},{12,4},{4,0},{1,9},{9... | collective-permute-start | bytes 1769480 | tf_op jit(solution)/shard_map/ppermute | solution.py:101
  308.1 26.6 %collective-permute-start.56 = (bf16[192,1536]{1,0:T(8,128)(2,1)}, bf16[192,1536]{1,0:T(8,128)(2,1)}, u32[]{:S(2)}, u32[]{:S(2)}) collective-permute-start(bf16[192,1536]{1,0:T(8,128)(2,1)} %get-tuple-element.482), channel_id=1, source_target_pairs={{8,0},{16,8},{24,16},{28,24},{20,28},{12,20},{4,12},{0,4},{9,1},{1... | collective-permute-start | bytes 1769480 | tf_op jit(solution)/shard_map/ppermute | solution.py:101
  309.5 25.2 %collective-permute-start.57 = (bf16[256,1536]{1,0:T(8,128)(2,1)}, bf16[256,1536]{1,0:T(8,128)(2,1)}, u32[]{:S(2)}, u32[]{:S(2)}) collective-permute-start(bf16[256,1536]{1,0:T(8,128)(2,1)} %get-tuple-element.483), channel_id=1, source_target_pairs={{0,1},{1,0},{2,3},{3,2},{4,5},{5,4},{6,7},{7,6},{8,9},{9,8},{10,11... | collective-permute-start | bytes 2359304 | tf_op jit(solution)/shard_map/ppermute | solution.py:101
  310.0 24.6 %collective-permute-start.58 = (bf16[96,384]{1,0:T(8,128)(2,1)}, bf16[96,384]{1,0:T(8,128)(2,1)}, u32[]{:S(2)}, u32[]{:S(2)}) collective-permute-start(bf16[96,384]{1,0:T(8,128)(2,1)} %get-tuple-element.484), channel_id=1, source_target_pairs={{0,8},{8,16},{16,24},{24,28},{28,20},{20,12},{12,4},{4,0},{1,9},{9... | collective-permute-start | bytes 221192 | tf_op jit(solution)/shard_map/ppermute | solution.py:101
  310.4 24.2 %collective-permute-start.59 = (bf16[96,384]{1,0:T(8,128)(2,1)S(1)}, bf16[96,384]{1,0:T(8,128)(2,1)}, u32[]{:S(2)}, u32[]{:S(2)}) collective-permute-start(bf16[96,384]{1,0:T(8,128)(2,1)S(1)} %get-tuple-element.485), channel_id=1, source_target_pairs={{8,0},{16,8},{24,16},{28,24},{20,28},{12,20},{4,12},{0,4},{9,1},{1... | collective-permute-start | bytes 221192 | tf_op jit(solution)/shard_map/ppermute | solution.py:101
  339.4 27.0 %collective-permute-start.60 = (bf16[192,1536]{1,0:T(8,128)(2,1)}, bf16[192,1536]{1,0:T(8,128)(2,1)}, u32[]{:S(2)}, u32[]{:S(2)}) collective-permute-start(bf16[192,1536]{1,0:T(8,128)(2,1)} %get-tuple-element.510), channel_id=1, source_target_pairs={{0,8},{8,16},{16,24},{24,28},{28,20},{20,12},{12,4},{4,0},{1,9},{9... | collective-permute-start | bytes 1769480 | tf_op jit(solution)/shard_map/ppermute | solution.py:101
  339.8 26.6 %collective-permute-start.61 = (bf16[192,1536]{1,0:T(8,128)(2,1)}, bf16[192,1536]{1,0:T(8,128)(2,1)}, u32[]{:S(2)}, u32[]{:S(2)}) collective-permute-start(bf16[192,1536]{1,0:T(8,128)(2,1)} %get-tuple-element.511), channel_id=1, source_target_pairs={{8,0},{16,8},{24,16},{28,24},{20,28},{12,20},{4,12},{0,4},{9,1},{1... | collective-permute-start | bytes 1769480 | tf_op jit(solution)/shard_map/ppermute | solution.py:101
  341.4 24.9 %collective-permute-start.62 = (bf16[192,384]{1,0:T(8,128)(2,1)}, bf16[192,384]{1,0:T(8,128)(2,1)}, u32[]{:S(2)}, u32[]{:S(2)}) collective-permute-start(bf16[192,384]{1,0:T(8,128)(2,1)} %pad_maximum_fusion.8), channel_id=1, source_target_pairs={{0,8},{8,16},{16,24},{24,28},{28,20},{20,12},{12,4},{4,0},{1,9},{9... | collective-permute-start | bytes 442376 | tf_op jit(solution)/shard_map/ppermute | solution.py:101
  341.9 24.5 %collective-permute-start.63 = (bf16[192,384]{1,0:T(8,128)(2,1)S(1)}, bf16[192,384]{1,0:T(8,128)(2,1)}, u32[]{:S(2)}, u32[]{:S(2)}) collective-permute-start(bf16[192,384]{1,0:T(8,128)(2,1)S(1)} %pad_maximum_fusion.9), channel_id=1, source_target_pairs={{8,0},{16,8},{24,16},{28,24},{20,28},{12,20},{4,12},{0,4},{9,1},{1... | collective-permute-start | bytes 442376 | tf_op jit(solution)/shard_map/ppermute | solution.py:101
  420.5 20.9 %collective-permute-start.76 = (bf16[512,1536]{1,0:T(8,128)(2,1)}, bf16[512,1536]{1,0:T(8,128)(2,1)S(1)}, u32[]{:S(2)}, u32[]{:S(2)}) collective-permute-start(bf16[512,1536]{1,0:T(8,128)(2,1)} %slice_bitcast_fusion.1), channel_id=1, source_target_pairs={{0,2},{2,0},{1,3},{3,1},{4,6},{6,4},{5,7},{7,5},{8,10},{10,8},{9,1... | collective-permute-start | bytes 4718600 | tf_op jit(solution)/shard_map/ppermute | solution.py:101
  421.4 19.9 %collective-permute-start.75 = (bf16[256,1536]{1,0:T(8,128)(2,1)}, bf16[256,1536]{1,0:T(8,128)(2,1)S(1)}, u32[]{:S(2)}, u32[]{:S(2)}) collective-permute-start(bf16[256,1536]{1,0:T(8,128)(2,1)} %get-tuple-element.589), channel_id=1, source_target_pairs={{0,1},{1,0},{2,3},{3,2},{4,5},{5,4},{6,7},{7,6},{8,9},{9,8},{10,11... | collective-permute-start | bytes 2359304 | tf_op jit(solution)/shard_map/ppermute | solution.py:101
  434.0 18.5 %collective-permute-start.93 = (bf16[96,1536]{1,0:T(8,128)(2,1)S(1)}, bf16[96,1536]{1,0:T(8,128)(2,1)S(1)}, u32[]{:S(2)}, u32[]{:S(2)}) collective-permute-start(bf16[96,1536]{1,0:T(8,128)(2,1)S(1)} %pad_maximum_fusion.7), channel_id=1, source_target_pairs={{0,0},{1,2},{2,1},{3,3},{4,4},{5,6},{6,5},{7,7},{8,8},{9,10},{10,9... | collective-permute-start | bytes 884744 | tf_op jit(solution)/shard_map/ppermute | solution.py:1115
  479.5 20.8 %collective-permute-start.87 = (bf16[48,1920]{1,0:T(8,128)(2,1)S(1)}, bf16[48,1920]{1,0:T(8,128)(2,1)S(1)}, u32[]{:S(2)}, u32[]{:S(2)}) collective-permute-start(bf16[48,1920]{1,0:T(8,128)(2,1)S(1)} %get-tuple-element.608), channel_id=1, source_target_pairs={{0,1},{1,0},{2,3},{3,2},{4,5},{5,4},{6,7},{7,6},{8,9},{9,8},{10,11... | collective-permute-start | bytes 552968 | tf_op jit(solution)/shard_map/ppermute | solution.py:101
  481.1 19.2 %collective-permute-start.88 = (bf16[48,1920]{1,0:T(8,128)(2,1)S(1)}, bf16[48,1920]{1,0:T(8,128)(2,1)S(1)}, u32[]{:S(2)}, u32[]{:S(2)}) collective-permute-start(bf16[48,1920]{1,0:T(8,128)(2,1)S(1)} %get-tuple-element.609), channel_id=1, source_target_pairs={{0,2},{1,3},{2,0},{3,1},{4,6},{5,7},{6,4},{7,5},{8,10},{9,11},{10,... | collective-permute-start | bytes 552968 | tf_op jit(solution)/shard_map/ppermute | solution.py:101
  481.3 19.0 %collective-permute-start.89 = (bf16[48,1920]{1,0:T(8,128)(2,1)S(1)}, bf16[48,1920]{1,0:T(8,128)(2,1)S(1)}, u32[]{:S(2)}, u32[]{:S(2)}) collective-permute-start(bf16[48,1920]{1,0:T(8,128)(2,1)S(1)} %get-tuple-element.610), channel_id=1, source_target_pairs={{0,3},{1,2},{2,1},{3,0},{4,7},{5,6},{6,5},{7,4},{8,11},{9,10},{10,... | collective-permute-start | bytes 552968 | tf_op jit(solution)/shard_map/ppermute | solution.py:101
  (151 other events, 1325.0 us)
